TPU v7x, 128 devices: a whole 4x4x4 slice. The times are simulated.
128 devices in a mesh: ctx: 32 (over z, y, core), head: 4 (over x).
Axes of the slice: x: 4, y: 4, z: 4, core: 2. Of those that a mesh axis runs over, the one named last changes fastest.
Arguments:
- query: bfloat16 [8192, 8192], P('ctx', 'head'), may hold values from -5 to 5
- keys: bfloat16 [8192, 1024], P('ctx', 'head'), may hold values from -5 to 5
- values: bfloat16 [8192, 1024], P('ctx', 'head'), may hold values from -6 to 6
- out_saved: bfloat16 [8192, 8192], P('ctx', 'head'), may hold values from -4 to 4
- d_out: bfloat16 [8192, 8192], P('ctx', 'head'), may hold values from -6 to 6
- doc_ids: int32 [8192], P(('ctx', 'head')), may hold values from 0 to 4, as said below
- placement: int32 [32], replicated, may hold values from 0 to 31, as said below
- block_keys: int32 [32, 12], replicated, may hold values from 0 to 31, as said below
Outputs:
- grad_query: bfloat16 [8192, 8192], P('ctx', 'head')
- grad_keys: bfloat16 [8192, 1024], P('ctx', 'head')
- grad_values: bfloat16 [8192, 1024], P('ctx', 'head')
Inputs may be any that keep to these rules, and one draw needn't show every extreme that they name: `placement`: A permutation of the block positions. `doc_ids`: read in packed-sequence order (block placement[s] holds stored block s), ids start at 0, never fall, and rise by one at exactly 4 positions. `block_keys`: column 0 of row b is b; every other entry of row b lies between b - 24 and b; entries may repeat.
All inputs are finite; a program needn't handle non-finite values.
Results may differ from a plain program's by a relative error of at most 0.014.
Values may be sent and summed in bfloat16 or wider, within the bound.
No kernel may reach another device: no remote copies, remote signals or barrier semaphores. Data moves between devices by JAX's collectives and lax.ppermute only.
A program may use at most 128 MiB of HBM per device.

v0:
```python
import math

import jax
import jax.numpy as jnp
from jax import lax
from jax.experimental import pallas as pl
from jax.experimental.pallas import tpu as pltpu
from jax.sharding import PartitionSpec as P

HD = 128
BLOCK = 256
GROUP = 8
WIDE = GROUP * HD
SCALE = 1.0 / math.sqrt(HD)
FACTOR = SCALE * math.log2(math.e)
HIDE = -1e30
STAT_ROWS = 16
SMALL_QUERY = 240.0


def gray(n):
    return n ^ (n >> 1)


def index_of(corner, core):
    return (gray(corner >> 2) * 4 + gray(corner & 3)) * 2 + core


def across(array, bit, turn=0):
    pairs = [(index_of(n, core), index_of(n ^ (1 << bit), core ^ turn)) for n in range(16) for core in range(2)]
    return lax.ppermute(array, "ctx", pairs)


def swap(array):
    return lax.ppermute(array, "ctx", [(i, i ^ 1) for i in range(32)])


def dot(a, b, contract):
    return lax.dot_general(a, b, ((contract[:1], contract[1:]), ((), ())), preferred_element_type=jnp.float32)


def fold(op, array):
    while array.shape[0] > 1:
        half = array.shape[0] // 2
        array = op(array[:half], array[half:])
    return array[0]


def fill_bias(bias, starts, table, which, key_block):
    key_pos = key_block * BLOCK + lax.broadcasted_iota(jnp.int32, (BLOCK, BLOCK), 0)
    query_pos = table[3, which] * BLOCK + lax.broadcasted_iota(jnp.int32, (1, BLOCK), 1)
    seen = (key_pos >= starts[pl.ds(which, 1), :]) & (key_pos <= query_pos)
    bias[...] = jnp.where(seen, 0.0, HIDE)


def fill_starts(starts, firsts, table, bounds):
    for which in range(2):
        begin = table[3, which] * BLOCK
        pos = begin + lax.broadcasted_iota(jnp.int32, (1, BLOCK), 1)
        row = jnp.zeros((1, BLOCK), jnp.int32)
        first = jnp.int32(0)
        for k in range(4):
            edge = bounds[0, k]
            row = jnp.maximum(row, jnp.where(pos >= edge, edge, 0))
            first = jnp.maximum(first, jnp.where(begin >= edge, edge, 0))
        starts[pl.ds(which, 1), :] = row
        firsts[which] = first


def needed(table, firsts, which, j):
    return (table[1 + which, j] > 0) & (table[0, j] * BLOCK + BLOCK - 1 >= firsts[which])


def block_at(place):
    return pl.ds(pl.multiple_of(place * BLOCK, BLOCK), BLOCK)


def add_to_sums(table, firsts, small, places, keys, bias, starts, top, total, q_turned):
    def masked(s, c):
        return (s[c : c + 64] * FACTOR + bias[c : c + 64, :]).reshape(8, 8, BLOCK)

    def update_small(row, s):
        amount = total[row]
        for c in range(0, BLOCK, 64):
            amount = amount + fold(jnp.add, jnp.exp2(masked(s, c)))
        total[row] = amount

    def update_any(row, s):
        old, amount = top[row], total[row]
        for c in range(0, BLOCK, 64):
            part = masked(s, c)
            new = jnp.maximum(old, fold(jnp.maximum, part))
            weights = jnp.exp2(part - new[None])
            amount = amount * jnp.exp2(old - new) + fold(jnp.add, weights)
            old = new
        total[row] = amount
        top[row] = old

    def run(update):
        def one(t, carry):
            place, dc, which = places.start + t // 4, (t // 2) % 2, t % 2
            j = table[12 + dc, place] * 2 + dc

            @pl.when(needed(table, firsts, which, j))
            def _():
                fill_bias(bias, starts, table, which, table[0, j])
                k = keys[dc, block_at(place), :]
                early = {}
                for step in range(GROUP + 1):
                    if step < GROUP:
                        early[step] = dot(k, q_turned[which * GROUP + step], (1, 0))
                    if step >= 1:
                        update(which * GROUP + step - 1, early.pop(step - 1))

            return carry

        lax.fori_loop(0, 4 * len(places), one, 0)

    pl.when(small[0] == 1)(lambda: run(update_small))
    pl.when(small[0] == 0)(lambda: run(update_any))


def near_sums_kernel(
    table, bounds, small, q_turned, held0, held1, come0, come1, top, total, keys, bias, starts, firsts, sems
):
    half = 4 * BLOCK
    copies = [
        pltpu.make_async_copy(ref, keys.at[n % 2, pl.ds(n // 2 * half, half)], sems.at[n])
        for n, ref in enumerate((held0, held1, come0, come1))
    ]
    for copy in copies:
        copy.start()
    fill_starts(starts, firsts, table, bounds)
    top[...] = jnp.full(top.shape, jnp.where(small[0] == 1, 0.0, HIDE), jnp.float32)
    total[...] = jnp.zeros(total.shape, jnp.float32)
    for copy in copies:
        copy.wait()
    add_to_sums(table, firsts, small, range(8), keys, bias, starts, top, total, q_turned)


def pack_keys_kernel(placement, doc_ids, keys, values, k_mine, v_mine, k_other, v_other, edges, sems):
    me = lax.axis_index("ctx")
    core = lax.rem(me, 2)
    copies = []
    for n, (ref, mine, other) in enumerate(((keys, k_mine, k_other), (values, v_mine, v_other))):
        for part, (out, head) in enumerate(((other, 1 - core), (mine, core))):
            cols = pl.ds(pl.multiple_of(head * HD, HD), HD)
            copies.append(pltpu.make_async_copy(ref.at[:, cols], out, sems.at[2 * n + part]))
    for copy in copies:
        copy.start()
    begin = placement[me] * BLOCK + lax.axis_index("head") * 64
    lane = lax.broadcasted_iota(jnp.int32, (1, HD), 1)
    row = jnp.zeros((1, HD), jnp.int32)
    for k in range(4):
        count = jnp.sum((doc_ids[...] <= k).astype(jnp.int32), axis=1, keepdims=True)
        row = jnp.where(lane == k, jnp.where(count > 0, begin + count, 0), row)
    edges[...] = row
    for copy in copies:
        copy.wait()


def pack_queries_kernel(query, d_out, saved, other, sems):
    core = lax.rem(lax.axis_index("ctx"), 2)
    cols = pl.ds(pl.multiple_of((1 - core) * WIDE, WIDE), WIDE)
    copies = [
        pltpu.make_async_copy(ref.at[:, cols], other.at[n], sems.at[n])
        for n, ref in enumerate((query, d_out, saved))
    ]
    for copy in copies:
        copy.start()
    for copy in copies:
        copy.wait()


def prepare_kernel(query, d_out, saved, swapped, after, q_turned, d_turned, delta, small, own, sems):
    del after
    peak = jnp.zeros((1, BLOCK), jnp.float32)
    begin = pl.multiple_of(lax.rem(lax.axis_index("ctx"), 2) * WIDE, WIDE)
    copies = [
        pltpu.make_async_copy(ref.at[:, pl.ds(begin, WIDE)], own.at[n], sems.at[n])
        for n, ref in enumerate((query, d_out, saved))
    ]
    for copy in copies:
        copy.start()
    for which, source in ((1, swapped), (0, own)):
        if which == 0:
            for copy in copies:
                copy.wait()
        for h in range(GROUP):
            row = which * GROUP + h
            cols = pl.ds(h * HD, HD)
            turned = source[0, :, cols].T
            q_turned[row] = turned
            turned = turned.astype(jnp.float32)
            peak = jnp.maximum(peak, jnp.sum(turned * turned, axis=0, keepdims=True))
            turned = source[1, :, cols].T
            d_turned[row] = turned
            product = turned.astype(jnp.float32) * source[2, :, cols].T.astype(jnp.float32)
            delta[pl.ds(row, 1), :] = jnp.sum(product, axis=0, keepdims=True)
    small[0] = (jnp.max(peak) <= SMALL_QUERY).astype(jnp.int32)


def main_kernel(table, bounds, small, q_turned, d_turned, delta, top_near, total_near, *rest):
    gq = rest[16:18]
    keep, send = rest[18:22], rest[22:26]
    kv_all, grad_all, gq_all, top, total, lse, gq_out, held_sums, bias, key_turned, starts, firsts, sems = rest[26:]
    copies = [
        pltpu.make_async_copy(
            rest[4 * part + n].at[pl.ds(0, 4 * BLOCK)],
            kv_all.at[n, pl.ds(4 * part * BLOCK, 4 * BLOCK)],
            sems.at[4 * part + n],
        )
        for part in range(4)
        for n in range(4)
    ]
    early = (8, 9, 12, 13)
    for n in early:
        copies[n].start()
    for n in range(16):
        if n not in early:
            copies[n].start()
    fill_starts(starts, firsts, table, bounds)
    top[...] = top_near[...]
    total[...] = total_near[...]
    gq_all[...] = jnp.zeros(gq_all.shape, jnp.float32)
    grad_all[...] = jnp.zeros(grad_all.shape, jnp.bfloat16)
    for n in early:
        copies[n].wait()

    add_to_sums(table, firsts, small, range(8, 16), kv_all, bias, starts, top, total, q_turned)
    for row in range(2 * GROUP):
        best = jnp.max(top[row], axis=0, keepdims=True)
        amount = jnp.sum(total[row] * jnp.exp2(top[row] - best), axis=0, keepdims=True)
        lse[pl.ds(row, 1), :] = best + jnp.log2(amount)
    for n in range(16):
        if n not in early:
            copies[n].wait()

    def add_gradients(t, carry):
        j, which = t // 2, t % 2
        rel, dc = j // 2, j % 2

        @pl.when(needed(table, firsts, which, j))
        def _():
            again = (which == 1) & needed(table, firsts, 0, j)
            fill_bias(bias, starts, table, which, table[0, j])
            k = kv_all[dc, block_at(table[4 + dc, rel]), :]
            v = kv_all[2 + dc, block_at(table[6 + dc, rel]), :]

            @pl.when(jnp.logical_not(again))
            def _():
                key_turned[...] = k.T
                held_sums[...] = jnp.zeros(held_sums.shape, jnp.float32)

            turned = key_turned[...]

            def first(h):
                row = which * GROUP + h
                return dot(k, q_turned[row], (1, 0)), dot(v, d_turned[row], (1, 0))

            def middle(h, s, dp):
                row = which * GROUP + h
                p = jnp.exp2(s * FACTOR + bias[...] - lse[pl.ds(row, 1), :])
                ds = (p * (dp - delta[pl.ds(row, 1), :])).astype(jnp.bfloat16)
                return p.astype(jnp.bfloat16), ds

            early, late = {}, {}
            gk_sum, gv_sum = held_sums[0], held_sums[1]
            for step in range(GROUP + 2):
                if step < GROUP:
                    early[step] = first(step)
                h = step - 1
                if 0 <= h < GROUP:
                    late[h] = middle(h, *early.pop(h))
                h = step - 2
                if 0 <= h < GROUP:
                    row = which * GROUP + h
                    p, ds = late.pop(h)
                    gv_sum = gv_sum + dot(d_turned[row], p, (1, 1))
                    gk_sum = gk_sum + dot(q_turned[row], ds, (1, 1))
                    gq_all[row] += dot(turned, ds, (1, 0))
            held_sums[0], held_sums[1] = gk_sum, gv_sum
            grad_all[dc, table[8 + dc, rel]] = (gk_sum * SCALE).T.astype(jnp.bfloat16)
            grad_all[2 + dc, table[10 + dc, rel]] = gv_sum.T.astype(jnp.bfloat16)

        return carry

    lax.fori_loop(0, 64, add_gradients, 0)
    outs = []
    for n in range(4):
        outs.append(pltpu.make_async_copy(grad_all.at[n, pl.ds(8, 8)], send[n], sems.at[2 * n + 1]))
        outs.append(pltpu.make_async_copy(grad_all.at[n, pl.ds(0, 8)], keep[n], sems.at[2 * n]))
    for copy in outs:
        copy.start()
    for which in (1, 0):
        for h in range(GROUP):
            turned = (gq_all[which * GROUP + h] * SCALE).T.astype(jnp.bfloat16)
            gq_out[which, :, pl.ds(h * HD, HD)] = turned
        outs.append(pltpu.make_async_copy(gq_out.at[which], gq[which], sems.at[8 + which]))
        outs[-1].start()
    for copy in outs:
        copy.wait()


SMEM = pl.BlockSpec(memory_space=pltpu.SMEM)
VMEM = pl.BlockSpec(memory_space=pltpu.VMEM)
ANY = pl.BlockSpec(memory_space=pl.ANY)
HBM = pl.BlockSpec(memory_space=pltpu.HBM)
TURNED = jax.ShapeDtypeStruct((2 * GROUP, HD, BLOCK), jnp.bfloat16)


def in_hbm(*arrays):
    return [pltpu.with_memory_space_constraint(array, pltpu.HBM) for array in arrays]


def pack_keys(placement, doc_ids, keys, values):
    half = jax.ShapeDtypeStruct((BLOCK, HD), jnp.bfloat16)
    return pl.pallas_call(
        pack_keys_kernel,
        out_shape=[half] * 4 + [jax.ShapeDtypeStruct((1, HD), jnp.int32)],
        in_specs=[SMEM, VMEM, ANY, ANY],
        out_specs=[VMEM] * 5,
        scratch_shapes=[pltpu.SemaphoreType.DMA((4,))],
        cost_estimate=pl.CostEstimate(flops=1000, bytes_accessed=1 << 19, transcendentals=0),
        name="pack_keys",
    )(placement, doc_ids, keys, values)


def pack_queries(query, d_out, saved):
    return pl.pallas_call(
        pack_queries_kernel,
        out_shape=jax.ShapeDtypeStruct((3, BLOCK, WIDE), jnp.bfloat16),
        in_specs=[ANY] * 3,
        out_specs=VMEM,
        scratch_shapes=[pltpu.SemaphoreType.DMA((3,))],
        cost_estimate=pl.CostEstimate(flops=1000, bytes_accessed=3 << 20, transcendentals=0),
        name="pack_queries",
    )(*in_hbm(query, d_out, saved))


def prepare(query, d_out, saved, swapped, after):
    return pl.pallas_call(
        prepare_kernel,
        out_shape=[
            TURNED,
            TURNED,
            jax.ShapeDtypeStruct((2 * GROUP, BLOCK), jnp.float32),
            jax.ShapeDtypeStruct((1,), jnp.int32),
        ],
        in_specs=[ANY] * 3 + [VMEM, ANY],
        out_specs=[VMEM] * 3 + [SMEM],
        scratch_shapes=[pltpu.VMEM((3, BLOCK, WIDE), jnp.bfloat16), pltpu.SemaphoreType.DMA((3,))],
        compiler_params=pltpu.CompilerParams(vmem_limit_bytes=16 * 1024 * 1024),
        cost_estimate=pl.CostEstimate(flops=2_000_000, bytes_accessed=5 << 20, transcendentals=0),
        name="prepare",
    )(*in_hbm(query, d_out, saved), swapped, after)


def near_sums(table, bounds, small, q_turned, held, come):
    state = jax.ShapeDtypeStruct((2 * GROUP, 8, BLOCK), jnp.float32)
    return pl.pallas_call(
        near_sums_kernel,
        out_shape=[state, state],
        in_specs=[SMEM] * 3 + [VMEM] + [ANY] * 4,
        out_specs=[VMEM] * 2,
        scratch_shapes=[
            pltpu.VMEM((2, 8 * BLOCK, HD), jnp.bfloat16),
            pltpu.VMEM((BLOCK, BLOCK), jnp.float32),
            pltpu.VMEM((8, BLOCK), jnp.int32),
            pltpu.SMEM((2,), jnp.int32),
            pltpu.SemaphoreType.DMA((4,)),
        ],
        compiler_params=pltpu.CompilerParams(vmem_limit_bytes=12 * 1024 * 1024),
        cost_estimate=pl.CostEstimate(flops=1_000_000_000, bytes_accessed=2 << 20, transcendentals=8 << 20),
        name="near_sums",
    )(table, bounds, small, q_turned, *held[:2], *come[:2])


def gradients(table, bounds, small, turned, sums, blocks):
    part = jax.ShapeDtypeStruct((8, BLOCK, HD), jnp.bfloat16)
    return pl.pallas_call(
        main_kernel,
        out_shape=[jax.ShapeDtypeStruct((BLOCK, WIDE), jnp.bfloat16)] * 2
        + [part] * 4
        + [pltpu.HBM((8, BLOCK, HD), jnp.bfloat16)] * 4,
        in_specs=[SMEM] * 3 + [VMEM] * 5 + [ANY] * 16,
        out_specs=[ANY] * 6 + [HBM] * 4,
        scratch_shapes=[
            pltpu.VMEM((4, 16 * BLOCK, HD), jnp.bfloat16),
            pltpu.VMEM((4, 16, BLOCK, HD), jnp.bfloat16),
            pltpu.VMEM((2 * GROUP, HD, BLOCK), jnp.float32),
            pltpu.VMEM((2 * GROUP, 8, BLOCK), jnp.float32),
            pltpu.VMEM((2 * GROUP, 8, BLOCK), jnp.float32),
            pltpu.VMEM((2 * GROUP, BLOCK), jnp.float32),
            pltpu.VMEM((2, BLOCK, WIDE), jnp.bfloat16),
            pltpu.VMEM((2, HD, BLOCK), jnp.float32),
            pltpu.VMEM((BLOCK, BLOCK), jnp.float32),
            pltpu.VMEM((HD, BLOCK), jnp.bfloat16),
            pltpu.VMEM((8, BLOCK), jnp.int32),
            pltpu.SMEM((2,), jnp.int32),
            pltpu.SemaphoreType.DMA((16,)),
        ],
        compiler_params=pltpu.CompilerParams(vmem_limit_bytes=30 * 1024 * 1024),
        cost_estimate=pl.CostEstimate(flops=12_000_000_000, bytes_accessed=10 << 20, transcendentals=16 << 20),
        name="gradients",
    )(table, bounds, small, *turned, *sums, *blocks)


def gather(parts, edges):
    held = [part[None] for part in parts]
    for step in range(3):
        sent = list(held)
        if step > 0:
            rows = jnp.broadcast_to(pack_edges(edges)[None], (held[0].shape[0], STAT_ROWS, HD))
            sent[0] = jnp.concatenate([held[0], rows], axis=1)
        come = [across(sent[n], (n + step) % 4) for n in range(4)]
        if step == 0:
            edges = jnp.maximum(edges, across(edges, 0))
        else:
            edges = jnp.maximum(edges, unpack_edges(come[0]))
            come[0] = come[0][:, :BLOCK]
        if step < 2:
            held = [jnp.concatenate(pair, axis=0) for pair in zip(held, come)]
            held = lax.optimization_barrier(held)
    far_held = [across(held[n], (n + 3) % 4) for n in range(4)]
    far_come = [across(come[n], (n + 3) % 4) for n in range(4)]
    edges = jnp.maximum(edges, across(edges, 3))
    return [array.reshape(4 * BLOCK, HD) for array in held + come + far_held + far_come], edges


def pack_edges(edges):
    spare = jnp.zeros((STAT_ROWS - 2, HD), jnp.int32)
    return jnp.concatenate([edges // 128, edges % 128, spare], axis=0).astype(jnp.bfloat16)


def unpack_edges(array):
    rows = array[:1, BLOCK : BLOCK + 2].astype(jnp.float32)
    return (rows[:, 0] * 128 + rows[:, 1]).astype(jnp.int32)


def reduce(keep, send, late):
    for step in range(4):
        if step == 3:
            moved = swap(jnp.stack([keep[1], keep[3]]))
            keep = [keep[0], moved[0], keep[2], moved[1]]
        come = [across(array, (n + step) % 4, n % 2 if step == 3 else 0) for n, array in enumerate(send)]
        total = [
            (a.astype(jnp.float32) + b.astype(jnp.float32)).astype(jnp.bfloat16) for a, b in zip(keep, come)
        ]
        if step == 3:
            return [a[0] for a in total], late
        if step == 1:
            total[3], late = lax.optimization_barrier((total[3], late))
        half = total[0].shape[0] // 2
        keep, send = [a[:half] for a in total], [a[half:] for a in total]


def shards(query, keys, values, out_saved, d_out, doc_ids, placement, block_keys):
    me = lax.axis_index("ctx")
    core = me % 2
    z, y = me // 8, (me // 2) % 4

    k_mine, v_mine, k_other, v_other, edges = pack_keys(placement, doc_ids[None], keys, values)
    k_swap, v_swap = swap(k_other), swap(v_other)
    query, d_out, out_saved, _ = lax.optimization_barrier((query, d_out, out_saved, k_other))
    swapped = swap(pack_queries(query, d_out, out_saved))
    edges, k_swap = lax.optimization_barrier((edges, k_swap))
    for_x = [lax.ppermute(edges, "head", [(i, (i + r) % 4) for i in range(4)]) for r in (1, 2, 3)]
    edges = jnp.maximum(jnp.maximum(edges, for_x[0]), jnp.maximum(for_x[1], for_x[2]))
    edges = jnp.maximum(edges, swap(edges))
    blocks, bounds = gather([k_mine, k_swap, v_mine, v_swap], edges)
    *turned, small = prepare(query, d_out, out_saved, swapped, blocks[1])

    j = jnp.arange(32)
    slots = index_of((gray(z) * 4 + gray(y)) ^ (j // 2), core ^ (j % 2))
    block_of = jnp.sum(jnp.where(slots[:, None] == jnp.arange(32)[None, :], placement[None, :], 0), axis=1)
    own = block_of[:2]
    chosen = jnp.sum(jnp.where(own[:, None, None] == jnp.arange(32)[None, :, None], block_keys[None], 0), axis=1)
    listed = jnp.any(chosen[:, :, None] == block_of[None, None, :], axis=1).astype(jnp.int32)
    bits = [[(rel >> bit) & 1 for bit in range(4)] for rel in range(32)]
    gathered = [[sum(b[(n + k) % 4] << k for k in range(4)) for b in bits] for n in range(4)]
    reduced = [[sum(b[(n + k) % 4] << (3 - k) for k in range(4)) for b in bits] for n in range(4)]
    order = [[gathered[n].index(place % 16) for place in range(32)] for n in range(2)]
    table = jnp.concatenate(
        [block_of[None], listed, block_of[None], jnp.array(gathered), jnp.array(reduced), jnp.array(order)], axis=0
    ).astype(jnp.int32)

    sums = near_sums(table, bounds, small, turned[0], blocks[0:4], blocks[4:8])
    outs = gradients(table, bounds, small, turned, sums, blocks)
    (gk_mine, gk_other, gv_mine, gv_other), gq_other = reduce(outs[2:6], outs[6:10], outs[1])

    def side_by_side(mine, other):
        return jnp.where(
            core == 0, jnp.concatenate([mine, other], axis=1), jnp.concatenate([other, mine], axis=1)
        )

    return (
        side_by_side(outs[0], swap(gq_other)),
        side_by_side(gk_mine, gk_other),
        side_by_side(gv_mine, gv_other),
    )


def solution(mesh):
    placed = (
        P("ctx", "head"),
        P("ctx", "head"),
        P("ctx", "head"),
        P("ctx", "head"),
        P("ctx", "head"),
        P(("ctx", "head")),
        P(),
        P(),
    )
    return jax.shard_map(
        shards,
        mesh=mesh,
        in_specs=placed,
        out_specs=(P("ctx", "head"), P("ctx", "head"), P("ctx", "head")),
        check_vma=False,
    )
```

profile of v0, /device:TPU:0, one launch (start us, length us, event | category | flops | bytes accessed | tf_op | source)
XLA Modules:
  0.0 133.5 jit_solution(2897798713386131971)
XLA Ops:
  0.6 2.3 %pack_keys.1 = (bf16[256,128]{1,0:T(8,128)(2,1)}, bf16[256,128]{1,0:T(8,128)(2,1)}, bf16[256,128]{1,0:T(8,128)(2,1)}, bf16[256,128]{1,0:T(8,128)(2,1)}, s32[1,128]{1,0:T(1,128)}) custom-call(s32[32]{0:T(128)} %placement.1, s32[1,64]{1,0:T(1,128)} %bitcast.73, bf16[256,256]{1,0:T(8,128)(2,1)} %keys.1, bf16[256,256]{1,0:T(8,128)(2,1)} %values.1), custom_call_target="tpu_custom_call" | custom-call | flops 1000 | bytes 524288 | tf_op jit(solution)/shard_map/pack_keys/pallas_call | solution.py:318
  3.6 1.7 %collective-permute-start.6 = (bf16[1,256,128]{2,1,0:T(8,128)(2,1)}, bf16[1,256,128]{2,1,0:T(8,128)(2,1)S(1)}, u32[]{:S(2)}, u32[]{:S(2)}) collective-permute-start(bf16[1,256,128]{2,1,0:T(8,128)(2,1)} %bitcast.68), channel_id=1, source_target_pairs={{0,8},{4,12},{8,0},{12,4},{24,16},{28,20},{16,24},{20,28},{32,40},... | collective-permute-start | bytes 196616 | tf_op jit(solution)/shard_map/ppermute | solution.py:31
  5.3 2.8 %collective-permute-start.3 = (s32[1,128]{1,0:T(1,128)}, s32[1,128]{1,0:T(1,128)S(1)}, u32[]{:S(2)}, u32[]{:S(2)}) collective-permute-start(s32[1,128]{1,0:T(1,128)} %get-tuple-element.41), channel_id=1, source_target_pairs={{0,3},{1,0},{2,1},{3,2},{4,7},{5,4},{6,5},{7,6},{8,11},{9,8},{10,9... | collective-permute-start | bytes 1544 | tf_op jit(solution)/shard_map/ppermute | solution.py:468
  8.2 0.8 collective-permute-start.2
  9.0 0.9 collective-permute-start.1
  9.8 2.5 %pack_queries.1 = bf16[3,256,1024]{2,1,0:T(8,128)(2,1)} custom-call(bf16[256,2048]{1,0:T(8,128)(2,1)} %query.1, bf16[256,2048]{1,0:T(8,128)(2,1)} %d_out.1, bf16[256,2048]{1,0:T(8,128)(2,1)} %saved.1), custom_call_target="tpu_custom_call" | custom-call | flops 1000 | bytes 3145728 | tf_op jit(solution)/shard_map/pack_queries/pallas_call | solution.py:330
  12.4 2.0 %collective-permute-start.8 = (bf16[1,256,128]{2,1,0:T(8,128)(2,1)S(1)}, bf16[1,256,128]{2,1,0:T(8,128)(2,1)S(1)}, u32[]{:S(2)}, u32[]{:S(2)}) collective-permute-start(bf16[1,256,128]{2,1,0:T(8,128)(2,1)S(1)} %bitcast.66), channel_id=1, source_target_pairs={{0,32},{4,36},{8,40},{12,44},{24,56},{28,60},{16,48},{20,52},{32,0... | collective-permute-start | bytes 196616 | tf_op jit(solution)/shard_map/ppermute | solution.py:31
  14.4 2.9 %collective-permute-start.10 = (bf16[1,256,128]{2,1,0:T(8,128)(2,1)S(1)}, bf16[1,256,128]{2,1,0:T(8,128)(2,1)S(1)}, u32[]{:S(2)}, u32[]{:S(2)}) collective-permute-start(bf16[1,256,128]{2,1,0:T(8,128)(2,1)S(1)} %bitcast.64), channel_id=1, source_target_pairs={{0,96},{4,100},{8,104},{12,108},{24,120},{28,124},{16,112},{20,116... | collective-permute-start | bytes 196616 | tf_op jit(solution)/shard_map/ppermute | solution.py:31
  17.3 2.2 %collective-permute-start.7 = (bf16[1,256,128]{2,1,0:T(8,128)(2,1)S(1)}, bf16[1,256,128]{2,1,0:T(8,128)(2,1)S(1)}, u32[]{:S(2)}, u32[]{:S(2)}) collective-permute-start(bf16[1,256,128]{2,1,0:T(8,128)(2,1)S(1)} %bitcast.62), channel_id=1, source_target_pairs={{0,24},{4,28},{8,16},{12,20},{24,0},{28,4},{16,8},{20,12},{32,56},... | collective-permute-start | bytes 196616 | tf_op jit(solution)/shard_map/ppermute | solution.py:31
  19.7 1.1 collective-permute-done.4
  21.4 2.9 %collective-permute-done.5 = s32[1,128]{1,0:T(1,128)S(1)} collective-permute-done((s32[1,128]{1,0:T(1,128)S(1)}, s32[1,128]{1,0:T(1,128)S(1)}, u32[]{:S(2)}, u32[]{:S(2)}) %collective-permute-start.5) | collective-permute-done | bytes 544 | tf_op jit(solution)/shard_map/ppermute | solution.py:31
  24.4 0.8 collective-permute-start.12
  26.6 2.6 %collective-permute-start.11 = (bf16[2,272,128]{2,1,0:T(8,128)(2,1)S(1)}, bf16[2,272,128]{2,1,0:T(8,128)(2,1)S(1)}, u32[]{:S(2)}, u32[]{:S(2)}) collective-permute-start(bf16[2,272,128]{2,1,0:T(8,128)(2,1)S(1)} %pad_maximum_fusion.5), channel_id=1, source_target_pairs={{0,24},{4,28},{8,16},{12,20},{24,0},{28,4},{16,8},{20,12},{32,56},... | collective-permute-start | bytes 417800 | tf_op jit(solution)/shard_map/ppermute | solution.py:31
  29.5 1.9 %collective-permute-done.13 = bf16[2,256,128]{2,1,0:T(8,128)(2,1)S(1)} collective-permute-done((bf16[2,256,128]{2,1,0:T(8,128)(2,1)S(1)}, bf16[2,256,128]{2,1,0:T(8,128)(2,1)S(1)}, u32[]{:S(2)}, u32[]{:S(2)}) %collective-permute-start.13) | collective-permute-done | bytes 131104 | tf_op jit(solution)/shard_map/ppermute | solution.py:31
  31.6 1.4 %collective-permute-done.11 = bf16[2,272,128]{2,1,0:T(8,128)(2,1)S(1)} collective-permute-done((bf16[2,272,128]{2,1,0:T(8,128)(2,1)S(1)}, bf16[2,272,128]{2,1,0:T(8,128)(2,1)S(1)}, u32[]{:S(2)}, u32[]{:S(2)}) %collective-permute-start.11) | collective-permute-done | bytes 139296 | tf_op jit(solution)/shard_map/ppermute | solution.py:31
  34.6 2.5 %collective-permute-start.21 = (bf16[4,256,128]{2,1,0:T(8,128)(2,1)S(1)}, bf16[4,256,128]{2,1,0:T(8,128)(2,1)S(1)}, u32[]{:S(2)}, u32[]{:S(2)}) collective-permute-start(bf16[4,256,128]{2,1,0:T(8,128)(2,1)S(1)} %pad_maximum_fusion.1), channel_id=1, source_target_pairs={{0,96},{4,100},{8,104},{12,108},{24,120},{28,124},{16,112},{20,116... | collective-permute-start | bytes 786440 | tf_op jit(solution)/shard_map/ppermute | solution.py:31
  38.3 2.5 %collective-permute-done.15 = bf16[4,272,128]{2,1,0:T(8,128)(2,1)} collective-permute-done((bf16[4,272,128]{2,1,0:T(8,128)(2,1)}, bf16[4,272,128]{2,1,0:T(8,128)(2,1)}, u32[]{:S(2)}, u32[]{:S(2)}) %collective-permute-start.15) | collective-permute-done | bytes 278560 | tf_op jit(solution)/shard_map/ppermute | solution.py:31
  40.8 2.6 %collective-permute-start.23 = (bf16[4,256,128]{2,1,0:T(8,128)(2,1)S(1)}, bf16[4,256,128]{2,1,0:T(8,128)(2,1)S(1)}, u32[]{:S(2)}, u32[]{:S(2)}) collective-permute-start(bf16[4,256,128]{2,1,0:T(8,128)(2,1)S(1)} %pad_maximum_fusion.3), channel_id=1, source_target_pairs={{0,24},{4,28},{8,16},{12,20},{24,0},{28,4},{16,8},{20,12},{32,56},... | collective-permute-start | bytes 786440 | tf_op jit(solution)/shard_map/ppermute | solution.py:31
  44.0 1.1 collective-permute-start.19
  45.1 1.0 collective-permute-start.20
  46.8 2.3 %collective-permute-start.16 = (s32[1,128]{1,0:T(1,128)S(1)}, s32[1,128]{1,0:T(1,128)S(1)}, u32[]{:S(2)}, u32[]{:S(2)}) collective-permute-start(s32[1,128]{1,0:T(1,128)S(1)} %bitcast_maximum_fusion), channel_id=1, source_target_pairs={{0,96},{4,100},{8,104},{12,108},{24,120},{28,124},{16,112},{20,116... | collective-permute-start | bytes 1544 | tf_op jit(solution)/shard_map/ppermute | solution.py:31
  49.2 1.0 slice.143
  51.5 1.6 %collective-permute-start.26 = (bf16[4,256,128]{2,1,0:T(8,128)(2,1)}, bf16[4,256,128]{2,1,0:T(8,128)(2,1)}, u32[]{:S(2)}, u32[]{:S(2)}) collective-permute-start(bf16[4,256,128]{2,1,0:T(8,128)(2,1)} %collective-permute-done.18), channel_id=1, source_target_pairs={{0,8},{4,12},{8,0},{12,4},{24,16},{28,20},{16,24},{20,28},{32,40},... | collective-permute-start | bytes 786440 | tf_op jit(solution)/shard_map/ppermute | solution.py:31
  53.0 1.0 collective-permute-done.20
  54.1 1.2 collective-permute-start.27
  55.3 1.4 %collective-permute-start.25 = (bf16[4,256,128]{2,1,0:T(8,128)(2,1)S(1)}, bf16[4,256,128]{2,1,0:T(8,128)(2,1)}, u32[]{:S(2)}, u32[]{:S(2)}) collective-permute-start(bf16[4,256,128]{2,1,0:T(8,128)(2,1)S(1)} %slice.143), channel_id=1, source_target_pairs={{0,96},{4,100},{8,104},{12,108},{24,120},{28,124},{16,112},{20,116... | collective-permute-start | bytes 786440 | tf_op jit(solution)/shard_map/ppermute | solution.py:31
  57.3 2.9 %prepare.1 = (bf16[16,128,256]{2,1,0:T(8,128)(2,1)S(1)}, bf16[16,128,256]{2,1,0:T(8,128)(2,1)S(1)}, f32[16,256]{1,0:T(8,128)S(1)}, s32[1]{0:T(128)}) custom-call(bf16[256,2048]{1,0:T(8,128)(2,1)} %query.1, bf16[256,2048]{1,0:T(8,128)(2,1)} %d_out.1, bf16[256,2048]{1,0:T(8,128)(2,1)} %saved.1, bf16[3,256,1024]{2,1,0:T(8,128)(2,1)S(1)} %collective-permute-done.17.swapped, ...), custom_call_target="tpu_custom_call" | custom-call | flops 2000000 | bytes 5242880 | tf_op jit(solution)/shard_map/prepare/pallas_call | solution.py:342
  60.2 5.6 %near_sums.1 = (f32[16,8,256]{2,1,0:T(8,128)S(1)}, f32[16,8,256]{2,1,0:T(8,128)S(1)}) custom-call(s32[14,32]{1,0:T(8,128)S(1)} %concatenate.69.table, s32[1,128]{1,0:T(1,128)S(1)} %max.31.bounds, s32[1]{0:T(128)} %get-tuple-element.55.small, bf16[16,128,256]{2,1,0:T(8,128)(2,1)S(1)} %get-tuple-element.56.q_turned, bf16[1024,128]{1,0:T(8,128)(2,1)S(1)} %bitcast.53, ...), custom_call_target="tpu_custom_call" | custom-call | flops 1000000000 | bytes 2097152 | tf_op jit(solution)/shard_map/near_sums/pallas_call | solution.py:361
  65.9 0.9 copy-done.3
  66.9 10.7 %gradients.1 = (bf16[256,1024]{1,0:T(8,128)(2,1)S(1)}, bf16[256,1024]{1,0:T(8,128)(2,1)S(1)}, bf16[8,256,128]{2,1,0:T(8,128)(2,1)S(1)}, bf16[8,256,128]{2,1,0:T(...) custom-call(s32[14,32]{1,0:T(8,128)S(1)} %concatenate.69.table, ...), custom_call_target="tpu_custom_call" | custom-call | flops 12000000000 | bytes 10485760 | tf_op jit(solution)/shard_map/gradients/pallas_call | solution.py:381
  77.6 0.8 copy-done.4
  78.4 1.9 %collective-permute-start.29 = (bf16[8,256,128]{2,1,0:T(8,128)(2,1)}, bf16[8,256,128]{2,1,0:T(8,128)(2,1)S(1)}, u32[]{:S(2)}, u32[]{:S(2)}) collective-permute-start(bf16[8,256,128]{2,1,0:T(8,128)(2,1)} %get-tuple-element.65), channel_id=1, source_target_pairs={{0,96},{4,100},{8,104},{12,108},{24,120},{28,124},{16,112},{20,116... | collective-permute-start | bytes 1572872 | tf_op jit(solution)/shard_map/ppermute | solution.py:31
  80.3 8.6 %collective-permute-start.32 = (bf16[8,256,128]{2,1,0:T(8,128)(2,1)}, bf16[8,256,128]{2,1,0:T(8,128)(2,1)}, u32[]{:S(2)}, u32[]{:S(2)}) collective-permute-start(bf16[8,256,128]{2,1,0:T(8,128)(2,1)} %get-tuple-element.69), channel_id=1, source_target_pairs={{0,8},{4,12},{8,0},{12,4},{24,16},{28,20},{16,24},{20,28},{32,40},... | collective-permute-start | bytes 1572872 | tf_op jit(solution)/shard_map/ppermute | solution.py:31
  88.9 5.2 %collective-permute-start.36 = (bf16[8,256,128]{2,1,0:T(8,128)(2,1)}, bf16[8,256,128]{2,1,0:T(8,128)(2,1)S(1)}, u32[]{:S(2)}, u32[]{:S(2)}) collective-permute-start(bf16[8,256,128]{2,1,0:T(8,128)(2,1)} %get-tuple-element.71), channel_id=1, source_target_pairs={{0,24},{4,28},{8,16},{12,20},{24,0},{28,4},{16,8},{20,12},{32,56},... | collective-permute-start | bytes 1572872 | tf_op jit(solution)/shard_map/ppermute | solution.py:31
  94.3 5.4 %collective-permute-start.30 = (bf16[4,256,128]{2,1,0:T(8,128)(2,1)S(1)}, bf16[4,256,128]{2,1,0:T(8,128)(2,1)S(1)}, u32[]{:S(2)}, u32[]{:S(2)}) collective-permute-start(bf16[4,256,128]{2,1,0:T(8,128)(2,1)S(1)} %slice.145), channel_id=1, source_target_pairs={{0,8},{4,12},{8,0},{12,4},{24,16},{28,20},{16,24},{20,28},{32,40},... | collective-permute-start | bytes 786440 | tf_op jit(solution)/shard_map/ppermute | solution.py:31
  99.8 1.2 add_convert_fusion.2
  101.0 5.7 %collective-permute-start.33 = (bf16[4,256,128]{2,1,0:T(8,128)(2,1)S(1)}, bf16[4,256,128]{2,1,0:T(8,128)(2,1)S(1)}, u32[]{:S(2)}, u32[]{:S(2)}) collective-permute-start(bf16[4,256,128]{2,1,0:T(8,128)(2,1)S(1)} %slice.147), channel_id=1, source_target_pairs={{0,24},{4,28},{8,16},{12,20},{24,0},{28,4},{16,8},{20,12},{32,56},... | collective-permute-start | bytes 786440 | tf_op jit(solution)/shard_map/ppermute | solution.py:31
  107.1 4.4 %collective-permute-start.43 = (bf16[4,256,128]{2,1,0:T(8,128)(2,1)S(1)}, bf16[4,256,128]{2,1,0:T(8,128)(2,1)S(1)}, u32[]{:S(2)}, u32[]{:S(2)}) collective-permute-start(bf16[4,256,128]{2,1,0:T(8,128)(2,1)S(1)} %slice.161), channel_id=1, source_target_pairs={{0,96},{4,100},{8,104},{12,108},{24,120},{28,124},{16,112},{20,116... | collective-permute-start | bytes 786440 | tf_op jit(solution)/shard_map/ppermute | solution.py:31
  111.9 1.5 %collective-permute-start.34 = (bf16[2,256,128]{2,1,0:T(8,128)(2,1)S(1)}, bf16[2,256,128]{2,1,0:T(8,128)(2,1)S(1)}, u32[]{:S(2)}, u32[]{:S(2)}) collective-permute-start(bf16[2,256,128]{2,1,0:T(8,128)(2,1)S(1)} %slice.149), channel_id=1, source_target_pairs={{0,32},{4,36},{8,40},{12,44},{24,56},{28,60},{16,48},{20,52},{32,0... | collective-permute-start | bytes 393224 | tf_op jit(solution)/shard_map/ppermute | solution.py:31
  113.5 5.7 %collective-permute-start.38 = (bf16[2,256,128]{2,1,0:T(8,128)(2,1)S(1)}, bf16[2,256,128]{2,1,0:T(8,128)(2,1)S(1)}, u32[]{:S(2)}, u32[]{:S(2)}) collective-permute-start(bf16[2,256,128]{2,1,0:T(8,128)(2,1)S(1)} %slice.155), channel_id=1, source_target_pairs={{0,96},{4,100},{8,104},{12,108},{24,120},{28,124},{16,112},{20,116... | collective-permute-start | bytes 393224 | tf_op jit(solution)/shard_map/ppermute | solution.py:31
  119.6 1.0 collective-permute-start.35
  120.6 1.5 %collective-permute-done.38 = bf16[2,256,128]{2,1,0:T(8,128)(2,1)S(1)} collective-permute-done((bf16[2,256,128]{2,1,0:T(8,128)(2,1)S(1)}, bf16[2,256,128]{2,1,0:T(8,128)(2,1)S(1)}, u32[]{:S(2)}, u32[]{:S(2)}) %collective-permute-start.38) | collective-permute-done | bytes 131104 | tf_op jit(solution)/shard_map/ppermute | solution.py:31
  122.2 1.2 collective-permute-start.41
  123.4 0.9 collective-permute-done.44
  124.4 0.8 collective-permute-done.35
  125.2 1.5 %collective-permute-start.45 = (bf16[1,256,128]{2,1,0:T(8,128)(2,1)S(1)}, bf16[1,256,128]{2,1,0:T(8,128)(2,1)S(1)}, u32[]{:S(2)}, u32[]{:S(2)}) collective-permute-start(bf16[1,256,128]{2,1,0:T(8,128)(2,1)S(1)} %slice.165), channel_id=1, source_target_pairs={{0,24},{4,28},{8,16},{12,20},{24,0},{28,4},{16,8},{20,12},{32,56},... | collective-permute-start | bytes 196616 | tf_op jit(solution)/shard_map/ppermute | solution.py:31
  126.7 4.0 %collective-permute-done.45 = bf16[1,256,128]{2,1,0:T(8,128)(2,1)S(1)} collective-permute-done((bf16[1,256,128]{2,1,0:T(8,128)(2,1)S(1)}, bf16[1,256,128]{2,1,0:T(8,128)(2,1)S(1)}, u32[]{:S(2)}, u32[]{:S(2)}) %collective-permute-start.45) | collective-permute-done | bytes 65568 | tf_op jit(solution)/shard_map/ppermute | solution.py:31
  132.1 1.4 %maximum_select_fusion = bf16[256,2048]{1,0:T(8,128)(2,1)} fusion(bf16[256,1024]{1,0:T(8,128)(2,1)S(1)} %collective-permute-done.31, bf16[256,1024]{1,0:T(8,128)(2,1)S(1)} %get-tuple-element.63, pred[]{:T(512)S(6)} %eq.57), kind=kLoop, calls=%fused_computation | loop fusion | flops 4718592 | bytes 2097153 | tf_op jit(solution)/shard_map/jit(_where)/select_n | solution.py:493
  (158 shorter events, 12.3 us)
Async XLA Ops:
  3.0 2.3 %collective-permute-start = (bf16[256,128]{1,0:T(8,128)(2,1)}, bf16[256,128]{1,0:T(8,128)(2,1)S(1)}, u32[]{:S(2)}, u32[]{:S(2)}) collective-permute-start(bf16[256,128]{1,0:T(8,128)(2,1)} %get-tuple-element.40), channel_id=1, source_target_pairs={{0,4},{4,0},{8,12},{12,8},{16,20},{20,16},{24,28},{28,24},{32,36},... | collective-permute-start | bytes 196616 | tf_op jit(solution)/shard_map/ppermute | solution.py:35
  3.1 9.3 %collective-permute-start.9 = (bf16[256,128]{1,0:T(8,128)(2,1)}, bf16[256,128]{1,0:T(8,128)(2,1)S(1)}, u32[]{:S(2)}, u32[]{:S(2)}) collective-permute-start(bf16[256,128]{1,0:T(8,128)(2,1)} %get-tuple-element.45), channel_id=1, source_target_pairs={{0,4},{4,0},{8,12},{12,8},{16,20},{20,16},{24,28},{28,24},{32,36},... | collective-permute-start | bytes 196616 | tf_op jit(solution)/shard_map/ppermute | solution.py:35
  3.6 16.0 %collective-permute-start.6 = (bf16[1,256,128]{2,1,0:T(8,128)(2,1)}, bf16[1,256,128]{2,1,0:T(8,128)(2,1)S(1)}, u32[]{:S(2)}, u32[]{:S(2)}) collective-permute-start(bf16[1,256,128]{2,1,0:T(8,128)(2,1)} %bitcast.68), channel_id=1, source_target_pairs={{0,8},{4,12},{8,0},{12,4},{24,16},{28,20},{16,24},{20,28},{32,40},... | collective-permute-start | bytes 196616 | tf_op jit(solution)/shard_map/ppermute | solution.py:31
  5.3 9.1 %collective-permute-start.3 = (s32[1,128]{1,0:T(1,128)}, s32[1,128]{1,0:T(1,128)S(1)}, u32[]{:S(2)}, u32[]{:S(2)}) collective-permute-start(s32[1,128]{1,0:T(1,128)} %get-tuple-element.41), channel_id=1, source_target_pairs={{0,3},{1,0},{2,1},{3,2},{4,7},{5,4},{6,5},{7,6},{8,11},{9,8},{10,9... | collective-permute-start | bytes 1544 | tf_op jit(solution)/shard_map/ppermute | solution.py:468
  8.2 6.2 %collective-permute-start.2 = (s32[1,128]{1,0:T(1,128)}, s32[1,128]{1,0:T(1,128)S(1)}, u32[]{:S(2)}, u32[]{:S(2)}) collective-permute-start(s32[1,128]{1,0:T(1,128)} %get-tuple-element.41), channel_id=1, source_target_pairs={{0,2},{1,3},{2,0},{3,1},{4,6},{5,7},{6,4},{7,5},{8,10},{9,11},{10,... | collective-permute-start | bytes 1544 | tf_op jit(solution)/shard_map/ppermute | solution.py:468
  9.0 8.3 %collective-permute-start.1 = (s32[1,128]{1,0:T(1,128)}, s32[1,128]{1,0:T(1,128)S(1)}, u32[]{:S(2)}, u32[]{:S(2)}) collective-permute-start(s32[1,128]{1,0:T(1,128)} %get-tuple-element.41), channel_id=1, source_target_pairs={{0,1},{1,2},{2,3},{3,0},{4,5},{5,6},{6,7},{7,4},{8,9},{9,10},{10,1... | collective-permute-start | bytes 1544 | tf_op jit(solution)/shard_map/ppermute | solution.py:468
  12.4 9.0 %collective-permute-start.8 = (bf16[1,256,128]{2,1,0:T(8,128)(2,1)S(1)}, bf16[1,256,128]{2,1,0:T(8,128)(2,1)S(1)}, u32[]{:S(2)}, u32[]{:S(2)}) collective-permute-start(bf16[1,256,128]{2,1,0:T(8,128)(2,1)S(1)} %bitcast.66), channel_id=1, source_target_pairs={{0,32},{4,36},{8,40},{12,44},{24,56},{28,60},{16,48},{20,52},{32,0... | collective-permute-start | bytes 196616 | tf_op jit(solution)/shard_map/ppermute | solution.py:31
  14.4 40.9 %collective-permute-start.17 = (bf16[3,256,1024]{2,1,0:T(8,128)(2,1)}, bf16[3,256,1024]{2,1,0:T(8,128)(2,1)S(1)}, u32[]{:S(2)}, u32[]{:S(2)}) collective-permute-start(bf16[3,256,1024]{2,1,0:T(8,128)(2,1)} %pack_queries.1), channel_id=1, source_target_pairs={{0,4},{4,0},{8,12},{12,8},{16,20},{20,16},{24,28},{28,24},{32,36},... | collective-permute-start | bytes 4718600 | tf_op jit(solution)/shard_map/ppermute | solution.py:35
  14.4 9.9 %collective-permute-start.10 = (bf16[1,256,128]{2,1,0:T(8,128)(2,1)S(1)}, bf16[1,256,128]{2,1,0:T(8,128)(2,1)S(1)}, u32[]{:S(2)}, u32[]{:S(2)}) collective-permute-start(bf16[1,256,128]{2,1,0:T(8,128)(2,1)S(1)} %bitcast.64), channel_id=1, source_target_pairs={{0,96},{4,100},{8,104},{12,108},{24,120},{28,124},{16,112},{20,116... | collective-permute-start | bytes 196616 | tf_op jit(solution)/shard_map/ppermute | solution.py:31
  17.3 7.1 %collective-permute-start.7 = (bf16[1,256,128]{2,1,0:T(8,128)(2,1)S(1)}, bf16[1,256,128]{2,1,0:T(8,128)(2,1)S(1)}, u32[]{:S(2)}, u32[]{:S(2)}) collective-permute-start(bf16[1,256,128]{2,1,0:T(8,128)(2,1)S(1)} %bitcast.62), channel_id=1, source_target_pairs={{0,24},{4,28},{8,16},{12,20},{24,0},{28,4},{16,8},{20,12},{32,56},... | collective-permute-start | bytes 196616 | tf_op jit(solution)/shard_map/ppermute | solution.py:31
  19.6 1.2 collective-permute-start.4
  20.8 3.5 %collective-permute-start.5 = (s32[1,128]{1,0:T(1,128)S(1)}, s32[1,128]{1,0:T(1,128)S(1)}, u32[]{:S(2)}, u32[]{:S(2)}) collective-permute-start(s32[1,128]{1,0:T(1,128)S(1)} %max.27), channel_id=1, source_target_pairs={{0,8},{4,12},{8,0},{12,4},{24,16},{28,20},{16,24},{20,28},{32,40},... | collective-permute-start | bytes 1544 | tf_op jit(solution)/shard_map/ppermute | solution.py:31
  24.4 5.0 %collective-permute-start.12 = (bf16[2,256,128]{2,1,0:T(8,128)(2,1)S(1)}, bf16[2,256,128]{2,1,0:T(8,128)(2,1)S(1)}, u32[]{:S(2)}, u32[]{:S(2)}) collective-permute-start(bf16[2,256,128]{2,1,0:T(8,128)(2,1)S(1)} %pad_maximum_fusion.7), channel_id=1, source_target_pairs={{0,32},{4,36},{8,40},{12,44},{24,56},{28,60},{16,48},{20,52},{32,0... | collective-permute-start | bytes 393224 | tf_op jit(solution)/shard_map/ppermute | solution.py:31
  25.3 6.2 %collective-permute-start.13 = (bf16[2,256,128]{2,1,0:T(8,128)(2,1)S(1)}, bf16[2,256,128]{2,1,0:T(8,128)(2,1)S(1)}, u32[]{:S(2)}, u32[]{:S(2)}) collective-permute-start(bf16[2,256,128]{2,1,0:T(8,128)(2,1)S(1)} %pad_maximum_fusion.8), channel_id=1, source_target_pairs={{0,96},{4,100},{8,104},{12,108},{24,120},{28,124},{16,112},{20,116... | collective-permute-start | bytes 393224 | tf_op jit(solution)/shard_map/ppermute | solution.py:31
  26.0 5.5 %collective-permute-start.14 = (bf16[2,256,128]{2,1,0:T(8,128)(2,1)S(1)}, bf16[2,256,128]{2,1,0:T(8,128)(2,1)S(1)}, u32[]{:S(2)}, u32[]{:S(2)}) collective-permute-start(bf16[2,256,128]{2,1,0:T(8,128)(2,1)S(1)} %pad_maximum_fusion.9), channel_id=1, source_target_pairs={{0,8},{4,12},{8,0},{12,4},{24,16},{28,20},{16,24},{20,28},{32,40},... | collective-permute-start | bytes 393224 | tf_op jit(solution)/shard_map/ppermute | solution.py:31
  26.6 6.3 %collective-permute-start.11 = (bf16[2,272,128]{2,1,0:T(8,128)(2,1)S(1)}, bf16[2,272,128]{2,1,0:T(8,128)(2,1)S(1)}, u32[]{:S(2)}, u32[]{:S(2)}) collective-permute-start(bf16[2,272,128]{2,1,0:T(8,128)(2,1)S(1)} %pad_maximum_fusion.5), channel_id=1, source_target_pairs={{0,24},{4,28},{8,16},{12,20},{24,0},{28,4},{16,8},{20,12},{32,56},... | collective-permute-start | bytes 417800 | tf_op jit(solution)/shard_map/ppermute | solution.py:31
  31.5 28.6 %copy-start = (bf16[4,256,128]{2,1,0:T(8,128)(2,1)}, bf16[4,256,128]{2,1,0:T(8,128)(2,1)S(1)}, u32[]{:S(2)}) copy-start(bf16[4,256,128]{2,1,0:T(8,128)(2,1)S(1)} %pad_maximum_fusion.4) | copy-start | bytes 786436
  33.9 6.9 %collective-permute-start.15 = (bf16[4,272,128]{2,1,0:T(8,128)(2,1)}, bf16[4,272,128]{2,1,0:T(8,128)(2,1)}, u32[]{:S(2)}, u32[]{:S(2)}) collective-permute-start(bf16[4,272,128]{2,1,0:T(8,128)(2,1)} %pad_maximum_fusion), channel_id=1, source_target_pairs={{0,32},{4,36},{8,40},{12,44},{24,56},{28,60},{16,48},{20,52},{32,0... | collective-permute-start | bytes 835592 | tf_op jit(solution)/shard_map/ppermute | solution.py:31
  34.6 9.4 %collective-permute-start.21 = (bf16[4,256,128]{2,1,0:T(8,128)(2,1)S(1)}, bf16[4,256,128]{2,1,0:T(8,128)(2,1)S(1)}, u32[]{:S(2)}, u32[]{:S(2)}) collective-permute-start(bf16[4,256,128]{2,1,0:T(8,128)(2,1)S(1)} %pad_maximum_fusion.1), channel_id=1, source_target_pairs={{0,96},{4,100},{8,104},{12,108},{24,120},{28,124},{16,112},{20,116... | collective-permute-start | bytes 786440 | tf_op jit(solution)/shard_map/ppermute | solution.py:31
  37.1 7.9 %collective-permute-start.22 = (bf16[4,256,128]{2,1,0:T(8,128)(2,1)S(1)}, bf16[4,256,128]{2,1,0:T(8,128)(2,1)S(1)}, u32[]{:S(2)}, u32[]{:S(2)}) collective-permute-start(bf16[4,256,128]{2,1,0:T(8,128)(2,1)S(1)} %pad_maximum_fusion.2), channel_id=1, source_target_pairs={{0,8},{4,12},{8,0},{12,4},{24,16},{28,20},{16,24},{20,28},{32,40},... | collective-permute-start | bytes 786440 | tf_op jit(solution)/shard_map/ppermute | solution.py:31
  37.5 9.3 %collective-permute-start.18 = (bf16[4,256,128]{2,1,0:T(8,128)(2,1)S(1)}, bf16[4,256,128]{2,1,0:T(8,128)(2,1)}, u32[]{:S(2)}, u32[]{:S(2)}) collective-permute-start(bf16[4,256,128]{2,1,0:T(8,128)(2,1)S(1)} %pad_maximum_fusion.2), channel_id=1, source_target_pairs={{0,96},{4,100},{8,104},{12,108},{24,120},{28,124},{16,112},{20,116... | collective-permute-start | bytes 786440 | tf_op jit(solution)/shard_map/ppermute | solution.py:31
  40.8 9.4 %collective-permute-start.23 = (bf16[4,256,128]{2,1,0:T(8,128)(2,1)S(1)}, bf16[4,256,128]{2,1,0:T(8,128)(2,1)S(1)}, u32[]{:S(2)}, u32[]{:S(2)}) collective-permute-start(bf16[4,256,128]{2,1,0:T(8,128)(2,1)S(1)} %pad_maximum_fusion.3), channel_id=1, source_target_pairs={{0,24},{4,28},{8,16},{12,20},{24,0},{28,4},{16,8},{20,12},{32,56},... | collective-permute-start | bytes 786440 | tf_op jit(solution)/shard_map/ppermute | solution.py:31
  44.0 7.4 %collective-permute-start.19 = (bf16[4,256,128]{2,1,0:T(8,128)(2,1)S(1)}, bf16[4,256,128]{2,1,0:T(8,128)(2,1)}, u32[]{:S(2)}, u32[]{:S(2)}) collective-permute-start(bf16[4,256,128]{2,1,0:T(8,128)(2,1)S(1)} %pad_maximum_fusion.3), channel_id=1, source_target_pairs={{0,8},{4,12},{8,0},{12,4},{24,16},{28,20},{16,24},{20,28},{32,40},... | collective-permute-start | bytes 786440 | tf_op jit(solution)/shard_map/ppermute | solution.py:31
  45.1 9.0 %collective-permute-start.20 = (bf16[4,256,128]{2,1,0:T(8,128)(2,1)S(1)}, bf16[4,256,128]{2,1,0:T(8,128)(2,1)}, u32[]{:S(2)}, u32[]{:S(2)}) collective-permute-start(bf16[4,256,128]{2,1,0:T(8,128)(2,1)S(1)} %pad_maximum_fusion.4), channel_id=1, source_target_pairs={{0,24},{4,28},{8,16},{12,20},{24,0},{28,4},{16,8},{20,12},{32,56},... | collective-permute-start | bytes 786440 | tf_op jit(solution)/shard_map/ppermute | solution.py:31
  46.8 8.5 %collective-permute-start.16 = (s32[1,128]{1,0:T(1,128)S(1)}, s32[1,128]{1,0:T(1,128)S(1)}, u32[]{:S(2)}, u32[]{:S(2)}) collective-permute-start(s32[1,128]{1,0:T(1,128)S(1)} %bitcast_maximum_fusion), channel_id=1, source_target_pairs={{0,96},{4,100},{8,104},{12,108},{24,120},{28,124},{16,112},{20,116... | collective-permute-start | bytes 1544 | tf_op jit(solution)/shard_map/ppermute | solution.py:31
  50.9 14.9 %collective-permute-start.24 = (bf16[4,256,128]{2,1,0:T(8,128)(2,1)S(1)}, bf16[4,256,128]{2,1,0:T(8,128)(2,1)}, u32[]{:S(2)}, u32[]{:S(2)}) collective-permute-start(bf16[4,256,128]{2,1,0:T(8,128)(2,1)S(1)} %pad_maximum_fusion.4), channel_id=1, source_target_pairs={{0,32},{4,36},{8,40},{12,44},{24,56},{28,60},{16,48},{20,52},{32,0... | collective-permute-start | bytes 786440 | tf_op jit(solution)/shard_map/ppermute | solution.py:31
  51.5 14.4 %collective-permute-start.26 = (bf16[4,256,128]{2,1,0:T(8,128)(2,1)}, bf16[4,256,128]{2,1,0:T(8,128)(2,1)}, u32[]{:S(2)}, u32[]{:S(2)}) collective-permute-start(bf16[4,256,128]{2,1,0:T(8,128)(2,1)} %collective-permute-done.18), channel_id=1, source_target_pairs={{0,8},{4,12},{8,0},{12,4},{24,16},{28,20},{16,24},{20,28},{32,40},... | collective-permute-start | bytes 786440 | tf_op jit(solution)/shard_map/ppermute | solution.py:31
  54.1 11.8 %collective-permute-start.27 = (bf16[4,256,128]{2,1,0:T(8,128)(2,1)}, bf16[4,256,128]{2,1,0:T(8,128)(2,1)}, u32[]{:S(2)}, u32[]{:S(2)}) collective-permute-start(bf16[4,256,128]{2,1,0:T(8,128)(2,1)} %collective-permute-done.19), channel_id=1, source_target_pairs={{0,24},{4,28},{8,16},{12,20},{24,0},{28,4},{16,8},{20,12},{32,56},... | collective-permute-start | bytes 786440 | tf_op jit(solution)/shard_map/ppermute | solution.py:31
  55.3 10.5 %collective-permute-start.28 = (bf16[4,256,128]{2,1,0:T(8,128)(2,1)}, bf16[4,256,128]{2,1,0:T(8,128)(2,1)}, u32[]{:S(2)}, u32[]{:S(2)}) collective-permute-start(bf16[4,256,128]{2,1,0:T(8,128)(2,1)} %collective-permute-done.20), channel_id=1, source_target_pairs={{0,32},{4,36},{8,40},{12,44},{24,56},{28,60},{16,48},{20,52},{32,0... | collective-permute-start | bytes 786440 | tf_op jit(solution)/shard_map/ppermute | solution.py:31
  55.3 10.5 %collective-permute-start.25 = (bf16[4,256,128]{2,1,0:T(8,128)(2,1)S(1)}, bf16[4,256,128]{2,1,0:T(8,128)(2,1)}, u32[]{:S(2)}, u32[]{:S(2)}) collective-permute-start(bf16[4,256,128]{2,1,0:T(8,128)(2,1)S(1)} %slice.143), channel_id=1, source_target_pairs={{0,96},{4,100},{8,104},{12,108},{24,120},{28,124},{16,112},{20,116... | collective-permute-start | bytes 786440 | tf_op jit(solution)/shard_map/ppermute | solution.py:31
  78.4 15.7 %collective-permute-start.29 = (bf16[8,256,128]{2,1,0:T(8,128)(2,1)}, bf16[8,256,128]{2,1,0:T(8,128)(2,1)S(1)}, u32[]{:S(2)}, u32[]{:S(2)}) collective-permute-start(bf16[8,256,128]{2,1,0:T(8,128)(2,1)} %get-tuple-element.65), channel_id=1, source_target_pairs={{0,96},{4,100},{8,104},{12,108},{24,120},{28,124},{16,112},{20,116... | collective-permute-start | bytes 1572872 | tf_op jit(solution)/shard_map/ppermute | solution.py:31
  80.3 19.4 %collective-permute-start.32 = (bf16[8,256,128]{2,1,0:T(8,128)(2,1)}, bf16[8,256,128]{2,1,0:T(8,128)(2,1)}, u32[]{:S(2)}, u32[]{:S(2)}) collective-permute-start(bf16[8,256,128]{2,1,0:T(8,128)(2,1)} %get-tuple-element.69), channel_id=1, source_target_pairs={{0,8},{4,12},{8,0},{12,4},{24,16},{28,20},{16,24},{20,28},{32,40},... | collective-permute-start | bytes 1572872 | tf_op jit(solution)/shard_map/ppermute | solution.py:31
  88.9 17.7 %collective-permute-start.36 = (bf16[8,256,128]{2,1,0:T(8,128)(2,1)}, bf16[8,256,128]{2,1,0:T(8,128)(2,1)S(1)}, u32[]{:S(2)}, u32[]{:S(2)}) collective-permute-start(bf16[8,256,128]{2,1,0:T(8,128)(2,1)} %get-tuple-element.71), channel_id=1, source_target_pairs={{0,24},{4,28},{8,16},{12,20},{24,0},{28,4},{16,8},{20,12},{32,56},... | collective-permute-start | bytes 1572872 | tf_op jit(solution)/shard_map/ppermute | solution.py:31
  94.1 12.8 %collective-permute-start.42 = (bf16[8,256,128]{2,1,0:T(8,128)(2,1)}, bf16[8,256,128]{2,1,0:T(8,128)(2,1)S(1)}, u32[]{:S(2)}, u32[]{:S(2)}) collective-permute-start(bf16[8,256,128]{2,1,0:T(8,128)(2,1)} %get-tuple-element.74), channel_id=1, source_target_pairs={{0,32},{4,36},{8,40},{12,44},{24,56},{28,60},{16,48},{20,52},{32,0... | collective-permute-start | bytes 1572872 | tf_op jit(solution)/shard_map/ppermute | solution.py:31
  94.3 17.2 %collective-permute-start.30 = (bf16[4,256,128]{2,1,0:T(8,128)(2,1)S(1)}, bf16[4,256,128]{2,1,0:T(8,128)(2,1)S(1)}, u32[]{:S(2)}, u32[]{:S(2)}) collective-permute-start(bf16[4,256,128]{2,1,0:T(8,128)(2,1)S(1)} %slice.145), channel_id=1, source_target_pairs={{0,8},{4,12},{8,0},{12,4},{24,16},{28,20},{16,24},{20,28},{32,40},... | collective-permute-start | bytes 786440 | tf_op jit(solution)/shard_map/ppermute | solution.py:31
  101.0 10.8 %collective-permute-start.33 = (bf16[4,256,128]{2,1,0:T(8,128)(2,1)S(1)}, bf16[4,256,128]{2,1,0:T(8,128)(2,1)S(1)}, u32[]{:S(2)}, u32[]{:S(2)}) collective-permute-start(bf16[4,256,128]{2,1,0:T(8,128)(2,1)S(1)} %slice.147), channel_id=1, source_target_pairs={{0,24},{4,28},{8,16},{12,20},{24,0},{28,4},{16,8},{20,12},{32,56},... | collective-permute-start | bytes 786440 | tf_op jit(solution)/shard_map/ppermute | solution.py:31
  106.8 6.6 %collective-permute-start.37 = (bf16[4,256,128]{2,1,0:T(8,128)(2,1)S(1)}, bf16[4,256,128]{2,1,0:T(8,128)(2,1)S(1)}, u32[]{:S(2)}, u32[]{:S(2)}) collective-permute-start(bf16[4,256,128]{2,1,0:T(8,128)(2,1)S(1)} %slice.153), channel_id=1, source_target_pairs={{0,32},{4,36},{8,40},{12,44},{24,56},{28,60},{16,48},{20,52},{32,0... | collective-permute-start | bytes 786440 | tf_op jit(solution)/shard_map/ppermute | solution.py:31
  107.1 12.1 %collective-permute-start.43 = (bf16[4,256,128]{2,1,0:T(8,128)(2,1)S(1)}, bf16[4,256,128]{2,1,0:T(8,128)(2,1)S(1)}, u32[]{:S(2)}, u32[]{:S(2)}) collective-permute-start(bf16[4,256,128]{2,1,0:T(8,128)(2,1)S(1)} %slice.161), channel_id=1, source_target_pairs={{0,96},{4,100},{8,104},{12,108},{24,120},{28,124},{16,112},{20,116... | collective-permute-start | bytes 786440 | tf_op jit(solution)/shard_map/ppermute | solution.py:31
  111.6 7.8 %collective-permute-start.39 = (bf16[2,256,128]{2,1,0:T(8,128)(2,1)S(1)}, bf16[2,256,128]{2,1,0:T(8,128)(2,1)S(1)}, u32[]{:S(2)}, u32[]{:S(2)}) collective-permute-start(bf16[2,256,128]{2,1,0:T(8,128)(2,1)S(1)} %slice.128), channel_id=1, source_target_pairs={{0,24},{4,28},{8,16},{12,20},{24,0},{28,4},{16,8},{20,12},{32,56},... | collective-permute-start | bytes 393224 | tf_op jit(solution)/shard_map/ppermute | solution.py:31
  111.7 20.4 %collective-permute-start.31 = (bf16[256,1024]{1,0:T(8,128)(2,1)S(1)}, bf16[256,1024]{1,0:T(8,128)(2,1)S(1)}, u32[]{:S(2)}, u32[]{:S(2)}) collective-permute-start(bf16[256,1024]{1,0:T(8,128)(2,1)S(1)} %copy-done.5), channel_id=1, source_target_pairs={{0,4},{4,0},{8,12},{12,8},{16,20},{20,16},{24,28},{28,24},{32,36},... | collective-permute-start | bytes 1572872 | tf_op jit(solution)/shard_map/ppermute | solution.py:35
  111.9 7.6 %collective-permute-start.34 = (bf16[2,256,128]{2,1,0:T(8,128)(2,1)S(1)}, bf16[2,256,128]{2,1,0:T(8,128)(2,1)S(1)}, u32[]{:S(2)}, u32[]{:S(2)}) collective-permute-start(bf16[2,256,128]{2,1,0:T(8,128)(2,1)S(1)} %slice.149), channel_id=1, source_target_pairs={{0,32},{4,36},{8,40},{12,44},{24,56},{28,60},{16,48},{20,52},{32,0... | collective-permute-start | bytes 393224 | tf_op jit(solution)/shard_map/ppermute | solution.py:31
  113.5 8.6 %collective-permute-start.38 = (bf16[2,256,128]{2,1,0:T(8,128)(2,1)S(1)}, bf16[2,256,128]{2,1,0:T(8,128)(2,1)S(1)}, u32[]{:S(2)}, u32[]{:S(2)}) collective-permute-start(bf16[2,256,128]{2,1,0:T(8,128)(2,1)S(1)} %slice.155), channel_id=1, source_target_pairs={{0,96},{4,100},{8,104},{12,108},{24,120},{28,124},{16,112},{20,116... | collective-permute-start | bytes 393224 | tf_op jit(solution)/shard_map/ppermute | solution.py:31
  119.3 5.0 %collective-permute-start.44 = (bf16[2,256,128]{2,1,0:T(8,128)(2,1)S(1)}, bf16[2,256,128]{2,1,0:T(8,128)(2,1)S(1)}, u32[]{:S(2)}, u32[]{:S(2)}) collective-permute-start(bf16[2,256,128]{2,1,0:T(8,128)(2,1)S(1)} %slice.163), channel_id=1, source_target_pairs={{0,8},{4,12},{8,0},{12,4},{24,16},{28,20},{16,24},{20,28},{32,40},... | collective-permute-start | bytes 393224 | tf_op jit(solution)/shard_map/ppermute | solution.py:31
  119.4 11.2 %collective-permute-start.46 = (bf16[1,256,128]{2,1,0:T(8,128)(2,1)S(1)}, bf16[1,256,128]{2,1,0:T(8,128)(2,1)S(1)}, u32[]{:S(2)}, u32[]{:S(2)}) collective-permute-start(bf16[1,256,128]{2,1,0:T(8,128)(2,1)S(1)} %get-tuple-element.81), channel_id=1, source_target_pairs={{0,36},{4,32},{8,44},{12,40},{24,60},{28,56},{16,52},{20,48},{32,4... | collective-permute-start | bytes 196616 | tf_op jit(solution)/shard_map/ppermute | solution.py:31
  119.6 5.6 %collective-permute-start.35 = (bf16[1,256,128]{2,1,0:T(8,128)(2,1)S(1)}, bf16[1,256,128]{2,1,0:T(8,128)(2,1)S(1)}, u32[]{:S(2)}, u32[]{:S(2)}) collective-permute-start(bf16[1,256,128]{2,1,0:T(8,128)(2,1)S(1)} %slice.151), channel_id=1, source_target_pairs={{0,96},{4,100},{8,104},{12,108},{24,120},{28,124},{16,112},{20,116... | collective-permute-start | bytes 196616 | tf_op jit(solution)/shard_map/ppermute | solution.py:31
  122.2 8.5 %collective-permute-start.41 = (bf16[1,256,128]{2,1,0:T(8,128)(2,1)S(1)}, bf16[1,256,128]{2,1,0:T(8,128)(2,1)S(1)}, u32[]{:S(2)}, u32[]{:S(2)}) collective-permute-start(bf16[1,256,128]{2,1,0:T(8,128)(2,1)S(1)} %get-tuple-element.84), channel_id=1, source_target_pairs={{0,12},{4,8},{8,4},{12,0},{24,20},{28,16},{16,28},{20,24},{32,44},... | collective-permute-start | bytes 196616 | tf_op jit(solution)/shard_map/ppermute | solution.py:31
  124.3 6.4 %collective-permute-start.40 = (bf16[2,1,256,128]{3,2,1,0:T(8,128)(2,1)S(1)}, bf16[2,1,256,128]{3,2,1,0:T(8,128)(2,1)S(1)}, u32[]{:S(2)}, u32[]{:S(2)}) collective-permute-start(bf16[2,1,256,128]{3,2,1,0:T(8,128)(2,1)S(1)} %pad_maximum_fusion.10), channel_id=1, source_target_pairs={{0,4},{4,0},{8,12},{12,8},{16,20},{20,16},{24,28},{28,24},{32,36},... | collective-permute-start | bytes 393224 | tf_op jit(solution)/shard_map/ppermute | solution.py:35
  125.2 5.5 %collective-permute-start.45 = (bf16[1,256,128]{2,1,0:T(8,128)(2,1)S(1)}, bf16[1,256,128]{2,1,0:T(8,128)(2,1)S(1)}, u32[]{:S(2)}, u32[]{:S(2)}) collective-permute-start(bf16[1,256,128]{2,1,0:T(8,128)(2,1)S(1)} %slice.165), channel_id=1, source_target_pairs={{0,24},{4,28},{8,16},{12,20},{24,0},{28,4},{16,8},{20,12},{32,56},... | collective-permute-start | bytes 196616 | tf_op jit(solution)/shard_map/ppermute | solution.py:31
  (19 other events, 228.0 us)
where the time goes:
time: 135 us; the launch traced here: 134 us
  starting transfers between devices  77.1 us (57%)
  Pallas kernels  24.1 us (18%)
  waiting for transfers between devices  19.6 us (15%)
  other arithmetic  7.35 us (5%)
  local copies, waits for them, and re-layouts  3.91 us (3%)
  between operations  1.4 us (1%)
    ppermute x38, starting transfers between devices, across(): return lax.ppermute(array, 'ctx', pairs)  71.9 us
    ppermute x38, waiting for transfers between devices, across(): return lax.ppermute(array, 'ctx', pairs)  18.6 us
    pallas_call x1, Pallas kernels, gradients(): pl.pallas_call(main_kernel, out_shape=[jax.ShapeDtypeStruct((BLOCK, WIDE)...  10.7 us
    pallas_call x1, Pallas kernels, near_sums(): pl.pallas_call(near_sums_kernel, out_shape=[state, state], in_specs=[SMEM...  5.6 us
    ppermute x3, starting transfers between devices, shards(): lax.ppermute(edges, 'head', [(i, (i + r) % 4) for i in range(4)])  4.51 us
    pallas_call x1, Pallas kernels, prepare(): pl.pallas_call(prepare_kernel, out_shape=[TURNED, TURNED, jax.ShapeDtypeS...  2.85 us
    select_n x3, other arithmetic, side_by_side(): jnp.where(core == 0, jnp.concatenate([mine, other], axis=1), jnp.concaten...  2.76 us
  transfers between devices with their start and end apart: 47, of which 13 were waited for; matrix products, arithmetic and copies ran while one was open for 5% of the time, Pallas kernels for 8%

commit v1 on v0

--- a/solution.py
+++ b/solution.py
@@ -380,11 +380,11 @@
     part = jax.ShapeDtypeStruct((8, BLOCK, HD), jnp.bfloat16)
     return pl.pallas_call(
         main_kernel,
-        out_shape=[jax.ShapeDtypeStruct((BLOCK, WIDE), jnp.bfloat16)] * 2
+        out_shape=[pltpu.HBM((BLOCK, WIDE), jnp.bfloat16)] * 2
         + [part] * 4
         + [pltpu.HBM((8, BLOCK, HD), jnp.bfloat16)] * 4,
         in_specs=[SMEM] * 3 + [VMEM] * 5 + [ANY] * 16,
-        out_specs=[ANY] * 6 + [HBM] * 4,
+        out_specs=[HBM] * 2 + [ANY] * 4 + [HBM] * 4,
         scratch_shapes=[
             pltpu.VMEM((4, 16 * BLOCK, HD), jnp.bfloat16),
             pltpu.VMEM((4, 16, BLOCK, HD), jnp.bfloat16),
@@ -438,7 +438,7 @@
     return (rows[:, 0] * 128 + rows[:, 1]).astype(jnp.int32)
 
 
-def reduce(keep, send, late):
+def reduce(keep, send, gq_mine, gq_other, side_by_side):
     for step in range(4):
         if step == 3:
             moved = swap(jnp.stack([keep[1], keep[3]]))
@@ -448,9 +448,12 @@
             (a.astype(jnp.float32) + b.astype(jnp.float32)).astype(jnp.bfloat16) for a, b in zip(keep, come)
         ]
         if step == 3:
-            return [a[0] for a in total], late
+            return [a[0] for a in total], gq
         if step == 1:
-            total[3], late = lax.optimization_barrier((total[3], late))
+            total[3], gq_other = lax.optimization_barrier((total[3], gq_other))
+            gq = side_by_side(gq_mine, swap(gq_other))
+        if step == 2:
+            total[3], gq = lax.optimization_barrier((total[3], gq))
         half = total[0].shape[0] // 2
         keep, send = [a[:half] for a in total], [a[half:] for a in total]
 
@@ -487,18 +490,13 @@
 
     sums = near_sums(table, bounds, small, turned[0], blocks[0:4], blocks[4:8])
     outs = gradients(table, bounds, small, turned, sums, blocks)
-    (gk_mine, gk_other, gv_mine, gv_other), gq_other = reduce(outs[2:6], outs[6:10], outs[1])
-
     def side_by_side(mine, other):
         return jnp.where(
             core == 0, jnp.concatenate([mine, other], axis=1), jnp.concatenate([other, mine], axis=1)
         )
 
-    return (
-        side_by_side(outs[0], swap(gq_other)),
-        side_by_side(gk_mine, gk_other),
-        side_by_side(gv_mine, gv_other),
-    )
+    (gk_mine, gk_other, gv_mine, gv_other), gq = reduce(outs[2:6], outs[6:10], *outs[:2], side_by_side)
+    return gq, side_by_side(gk_mine, gk_other), side_by_side(gv_mine, gv_other)
 
 
 def solution(mesh):

time: 135 us -> 127 us (0.941); the launches traced: 134 us -> 127 us
  starting transfers between devices: 77.1 us -> 69.7 us
  Pallas kernels: 24.1 us -> 28.5 us
  local copies, waits for them, and re-layouts: 3.91 us -> 2.12 us
    ppermute x38, starting transfers between devices: 71.9 us -> 64.3 us  [across(): return lax.ppermute(array, 'ctx', pairs)]
    pallas_call x1, Pallas kernels: 10.7 us -> 14.5 us  [gradients(): pl.pallas_call(main_kernel, out_shape=[pltpu.HBM((BLOCK, WIDE), jnp.bfloa...]
    unnamed x40 -> x32, local copies, waits for them, and re-layouts: 2.56 us -> 0.77 us
  transfers between devices with their start and end apart: 47 -> 47, of which waited for: 13 -> 17; matrix products, arithmetic and copies ran while one was open for 5% -> 5% of each run, Pallas kernels for 8% -> 9%
where the time goes in v1:
time: 127 us
  starting transfers between devices  69.7 us (55%)
  Pallas kernels  28.5 us (22%)
  waiting for transfers between devices  19.1 us (15%)
  other arithmetic  6.64 us (5%)
  local copies, waits for them, and re-layouts  2.12 us (2%)
  between operations  1.33 us (1%)
    ppermute x38, starting transfers between devices, across(): return lax.ppermute(array, 'ctx', pairs)  64.3 us
    ppermute x38, waiting for transfers between devices, across(): return lax.ppermute(array, 'ctx', pairs)  18 us
    pallas_call x1, Pallas kernels, gradients(): pl.pallas_call(main_kernel, out_shape=[pltpu.HBM((BLOCK, WIDE), jnp.bfloa...  14.5 us
    pallas_call x1, Pallas kernels, near_sums(): pl.pallas_call(near_sums_kernel, out_shape=[state, state], in_specs=[SMEM...  6.23 us
    ppermute x3, starting transfers between devices, shards(): lax.ppermute(edges, 'head', [(i, (i + r) % 4) for i in range(4)])  4.51 us
    pallas_call x1, Pallas kernels, prepare(): pl.pallas_call(prepare_kernel, out_shape=[TURNED, TURNED, jax.ShapeDtypeS...  2.85 us
    select_n x3, other arithmetic, side_by_side(): jnp.where(core == 0, jnp.concatenate([mine, other], axis=1), jnp.concaten...  2.76 us
    pallas_call x1, Pallas kernels, pack_queries(): pl.pallas_call(pack_queries_kernel, out_shape=jax.ShapeDtypeStruct((3, BL...  2.56 us
  transfers between devices with their start and end apart: 47, of which 17 were waited for; matrix products, arithmetic and copies ran while one was open for 5% of the time, Pallas kernels for 9%

profile of v1, /device:TPU:0, one launch (start us, length us, event | category | flops | bytes accessed | tf_op | source)
XLA Modules:
  0.0 127.4 jit_solution(10297279143886884039)
XLA Ops:
  0.6 2.3 %pack_keys.1 = (bf16[256,128]{1,0:T(8,128)(2,1)}, bf16[256,128]{1,0:T(8,128)(2,1)}, bf16[256,128]{1,0:T(8,128)(2,1)}, bf16[256,128]{1,0:T(8,128)(2,1)}, s32[1,128]{1,0:T(1,128)}) custom-call(s32[32]{0:T(128)} %placement.1, s32[1,64]{1,0:T(1,128)} %bitcast.73, bf16[256,256]{1,0:T(8,128)(2,1)} %keys.1, bf16[256,256]{1,0:T(8,128)(2,1)} %values.1), custom_call_target="tpu_custom_call" | custom-call | flops 1000 | bytes 524288 | tf_op jit(solution)/shard_map/pack_keys/pallas_call | solution.py:318
  3.6 1.7 %collective-permute-start.6 = (bf16[1,256,128]{2,1,0:T(8,128)(2,1)}, bf16[1,256,128]{2,1,0:T(8,128)(2,1)S(1)}, u32[]{:S(2)}, u32[]{:S(2)}) collective-permute-start(bf16[1,256,128]{2,1,0:T(8,128)(2,1)} %bitcast.68), channel_id=1, source_target_pairs={{0,8},{4,12},{8,0},{12,4},{24,16},{28,20},{16,24},{20,28},{32,40},... | collective-permute-start | bytes 196616 | tf_op jit(solution)/shard_map/ppermute | solution.py:31
  5.3 2.8 %collective-permute-start.3 = (s32[1,128]{1,0:T(1,128)}, s32[1,128]{1,0:T(1,128)S(1)}, u32[]{:S(2)}, u32[]{:S(2)}) collective-permute-start(s32[1,128]{1,0:T(1,128)} %get-tuple-element.43), channel_id=1, source_target_pairs={{0,3},{1,0},{2,1},{3,2},{4,7},{5,4},{6,5},{7,6},{8,11},{9,8},{10,9... | collective-permute-start | bytes 1544 | tf_op jit(solution)/shard_map/ppermute | solution.py:471
  8.2 0.8 collective-permute-start.2
  9.0 0.9 collective-permute-start.1
  9.8 2.6 %pack_queries.1 = bf16[3,256,1024]{2,1,0:T(8,128)(2,1)} custom-call(bf16[256,2048]{1,0:T(8,128)(2,1)} %query.1, bf16[256,2048]{1,0:T(8,128)(2,1)} %d_out.1, bf16[256,2048]{1,0:T(8,128)(2,1)} %saved.1), custom_call_target="tpu_custom_call" | custom-call | flops 1000 | bytes 3145728 | tf_op jit(solution)/shard_map/pack_queries/pallas_call | solution.py:330
  12.4 2.0 %collective-permute-start.8 = (bf16[1,256,128]{2,1,0:T(8,128)(2,1)S(1)}, bf16[1,256,128]{2,1,0:T(8,128)(2,1)S(1)}, u32[]{:S(2)}, u32[]{:S(2)}) collective-permute-start(bf16[1,256,128]{2,1,0:T(8,128)(2,1)S(1)} %bitcast.66), channel_id=1, source_target_pairs={{0,32},{4,36},{8,40},{12,44},{24,56},{28,60},{16,48},{20,52},{32,0... | collective-permute-start | bytes 196616 | tf_op jit(solution)/shard_map/ppermute | solution.py:31
  14.4 2.9 %collective-permute-start.10 = (bf16[1,256,128]{2,1,0:T(8,128)(2,1)S(1)}, bf16[1,256,128]{2,1,0:T(8,128)(2,1)S(1)}, u32[]{:S(2)}, u32[]{:S(2)}) collective-permute-start(bf16[1,256,128]{2,1,0:T(8,128)(2,1)S(1)} %bitcast.64), channel_id=1, source_target_pairs={{0,96},{4,100},{8,104},{12,108},{24,120},{28,124},{16,112},{20,116... | collective-permute-start | bytes 196616 | tf_op jit(solution)/shard_map/ppermute | solution.py:31
  17.3 2.2 %collective-permute-start.7 = (bf16[1,256,128]{2,1,0:T(8,128)(2,1)S(1)}, bf16[1,256,128]{2,1,0:T(8,128)(2,1)S(1)}, u32[]{:S(2)}, u32[]{:S(2)}) collective-permute-start(bf16[1,256,128]{2,1,0:T(8,128)(2,1)S(1)} %bitcast.62), channel_id=1, source_target_pairs={{0,24},{4,28},{8,16},{12,20},{24,0},{28,4},{16,8},{20,12},{32,56},... | collective-permute-start | bytes 196616 | tf_op jit(solution)/shard_map/ppermute | solution.py:31
  19.7 1.1 collective-permute-done.4
  21.4 2.9 %collective-permute-done.5 = s32[1,128]{1,0:T(1,128)S(1)} collective-permute-done((s32[1,128]{1,0:T(1,128)S(1)}, s32[1,128]{1,0:T(1,128)S(1)}, u32[]{:S(2)}, u32[]{:S(2)}) %collective-permute-start.5) | collective-permute-done | bytes 544 | tf_op jit(solution)/shard_map/ppermute | solution.py:31
  24.4 0.8 collective-permute-start.12
  25.3 0.7 collective-permute-start.13
  26.7 2.6 %collective-permute-start.11 = (bf16[2,272,128]{2,1,0:T(8,128)(2,1)S(1)}, bf16[2,272,128]{2,1,0:T(8,128)(2,1)S(1)}, u32[]{:S(2)}, u32[]{:S(2)}) collective-permute-start(bf16[2,272,128]{2,1,0:T(8,128)(2,1)S(1)} %pad_maximum_fusion.5), channel_id=1, source_target_pairs={{0,24},{4,28},{8,16},{12,20},{24,0},{28,4},{16,8},{20,12},{32,56},... | collective-permute-start | bytes 417800 | tf_op jit(solution)/shard_map/ppermute | solution.py:31
  29.5 2.0 %collective-permute-done.13 = bf16[2,256,128]{2,1,0:T(8,128)(2,1)S(1)} collective-permute-done((bf16[2,256,128]{2,1,0:T(8,128)(2,1)S(1)}, bf16[2,256,128]{2,1,0:T(8,128)(2,1)S(1)}, u32[]{:S(2)}, u32[]{:S(2)}) %collective-permute-start.13) | collective-permute-done | bytes 131104 | tf_op jit(solution)/shard_map/ppermute | solution.py:31
  31.6 1.5 %collective-permute-done.11 = bf16[2,272,128]{2,1,0:T(8,128)(2,1)S(1)} collective-permute-done((bf16[2,272,128]{2,1,0:T(8,128)(2,1)S(1)}, bf16[2,272,128]{2,1,0:T(8,128)(2,1)S(1)}, u32[]{:S(2)}, u32[]{:S(2)}) %collective-permute-start.11) | collective-permute-done | bytes 139296 | tf_op jit(solution)/shard_map/ppermute | solution.py:31
  33.2 0.7 collective-permute-start.15
  34.0 2.5 %collective-permute-start.21 = (bf16[4,256,128]{2,1,0:T(8,128)(2,1)S(1)}, bf16[4,256,128]{2,1,0:T(8,128)(2,1)S(1)}, u32[]{:S(2)}, u32[]{:S(2)}) collective-permute-start(bf16[4,256,128]{2,1,0:T(8,128)(2,1)S(1)} %pad_maximum_fusion.1), channel_id=1, source_target_pairs={{0,96},{4,100},{8,104},{12,108},{24,120},{28,124},{16,112},{20,116... | collective-permute-start | bytes 786440 | tf_op jit(solution)/shard_map/ppermute | solution.py:31
  36.9 0.8 collective-permute-start.18
  37.7 2.3 %collective-permute-done.15 = bf16[4,272,128]{2,1,0:T(8,128)(2,1)} collective-permute-done((bf16[4,272,128]{2,1,0:T(8,128)(2,1)S(1)}, bf16[4,272,128]{2,1,0:T(8,128)(2,1)}, u32[]{:S(2)}, u32[]{:S(2)}) %collective-permute-start.15) | collective-permute-done | bytes 278560 | tf_op jit(solution)/shard_map/ppermute | solution.py:31
  40.0 2.6 %collective-permute-start.23 = (bf16[4,256,128]{2,1,0:T(8,128)(2,1)S(1)}, bf16[4,256,128]{2,1,0:T(8,128)(2,1)S(1)}, u32[]{:S(2)}, u32[]{:S(2)}) collective-permute-start(bf16[4,256,128]{2,1,0:T(8,128)(2,1)S(1)} %pad_maximum_fusion.3), channel_id=1, source_target_pairs={{0,24},{4,28},{8,16},{12,20},{24,0},{28,4},{16,8},{20,12},{32,56},... | collective-permute-start | bytes 786440 | tf_op jit(solution)/shard_map/ppermute | solution.py:31
  43.3 1.2 collective-permute-start.19
  44.5 1.0 collective-permute-start.20
  46.2 2.3 %collective-permute-start.16 = (s32[1,128]{1,0:T(1,128)S(1)}, s32[1,128]{1,0:T(1,128)S(1)}, u32[]{:S(2)}, u32[]{:S(2)}) collective-permute-start(s32[1,128]{1,0:T(1,128)S(1)} %bitcast_maximum_fusion), channel_id=1, source_target_pairs={{0,96},{4,100},{8,104},{12,108},{24,120},{28,124},{16,112},{20,116... | collective-permute-start | bytes 1544 | tf_op jit(solution)/shard_map/ppermute | solution.py:31
  48.5 1.0 slice.143
  50.6 1.8 %collective-permute-start.26 = (bf16[4,256,128]{2,1,0:T(8,128)(2,1)}, bf16[4,256,128]{2,1,0:T(8,128)(2,1)}, u32[]{:S(2)}, u32[]{:S(2)}) collective-permute-start(bf16[4,256,128]{2,1,0:T(8,128)(2,1)} %collective-permute-done.18), channel_id=1, source_target_pairs={{0,8},{4,12},{8,0},{12,4},{24,16},{28,20},{16,24},{20,28},{32,40},... | collective-permute-start | bytes 786440 | tf_op jit(solution)/shard_map/ppermute | solution.py:31
  52.4 1.2 collective-permute-done.20
  53.6 0.9 collective-permute-start.27
  54.5 2.3 %collective-permute-start.25 = (bf16[4,256,128]{2,1,0:T(8,128)(2,1)S(1)}, bf16[4,256,128]{2,1,0:T(8,128)(2,1)}, u32[]{:S(2)}, u32[]{:S(2)}) collective-permute-start(bf16[4,256,128]{2,1,0:T(8,128)(2,1)S(1)} %slice.143), channel_id=1, source_target_pairs={{0,96},{4,100},{8,104},{12,108},{24,120},{28,124},{16,112},{20,116... | collective-permute-start | bytes 786440 | tf_op jit(solution)/shard_map/ppermute | solution.py:31
  57.4 2.9 %prepare.1 = (bf16[16,128,256]{2,1,0:T(8,128)(2,1)S(1)}, bf16[16,128,256]{2,1,0:T(8,128)(2,1)S(1)}, f32[16,256]{1,0:T(8,128)S(1)}, s32[1]{0:T(128)}) custom-call(bf16[256,2048]{1,0:T(8,128)(2,1)} %query.1, bf16[256,2048]{1,0:T(8,128)(2,1)} %d_out.1, bf16[256,2048]{1,0:T(8,128)(2,1)} %saved.1, bf16[3,256,1024]{2,1,0:T(8,128)(2,1)S(1)} %collective-permute-done.17.swapped, ...), custom_call_target="tpu_custom_call" | custom-call | flops 2000000 | bytes 5242880 | tf_op jit(solution)/shard_map/prepare/pallas_call | solution.py:342
  60.3 6.2 %near_sums.1 = (f32[16,8,256]{2,1,0:T(8,128)S(1)}, f32[16,8,256]{2,1,0:T(8,128)S(1)}) custom-call(s32[14,32]{1,0:T(8,128)S(1)} %concatenate.69.table, s32[1,128]{1,0:T(1,128)S(1)} %max.31.bounds, s32[1]{0:T(128)} %get-tuple-element.57.small, bf16[16,128,256]{2,1,0:T(8,128)(2,1)S(1)} %get-tuple-element.58.q_turned, bf16[1024,128]{1,0:T(8,128)(2,1)S(1)} %bitcast.53, ...), custom_call_target="tpu_custom_call" | custom-call | flops 1000000000 | bytes 2097152 | tf_op jit(solution)/shard_map/near_sums/pallas_call | solution.py:361
  66.7 14.5 %gradients.1 = (bf16[256,1024]{1,0:T(8,128)(2,1)}, bf16[256,1024]{1,0:T(8,128)(2,1)}, bf16[8,256,128]{2,1,0:T(8,128)(2,1)S(1)}, bf16[8,256,128]{2,1,0:T(8,128)(2...) custom-call(s32[14,32]{1,0:T(8,128)S(1)} %concatenate.69.table, ...), custom_call_target="tpu_custom_call" | custom-call | flops 12000000000 | bytes 10485760 | tf_op jit(solution)/shard_map/gradients/pallas_call | solution.py:381
  81.2 8.0 %collective-permute-start.33 = (bf16[8,256,128]{2,1,0:T(8,128)(2,1)}, bf16[8,256,128]{2,1,0:T(8,128)(2,1)S(1)}, u32[]{:S(2)}, u32[]{:S(2)}) collective-permute-start(bf16[8,256,128]{2,1,0:T(8,128)(2,1)} %get-tuple-element.73), channel_id=1, source_target_pairs={{0,8},{4,12},{8,0},{12,4},{24,16},{28,20},{16,24},{20,28},{32,40},... | collective-permute-start | bytes 1572872 | tf_op jit(solution)/shard_map/ppermute | solution.py:31
  89.3 2.2 %collective-permute-start.37 = (bf16[8,256,128]{2,1,0:T(8,128)(2,1)}, bf16[8,256,128]{2,1,0:T(8,128)(2,1)S(1)}, u32[]{:S(2)}, u32[]{:S(2)}) collective-permute-start(bf16[8,256,128]{2,1,0:T(8,128)(2,1)} %get-tuple-element.75), channel_id=1, source_target_pairs={{0,24},{4,28},{8,16},{12,20},{24,0},{28,4},{16,8},{20,12},{32,56},... | collective-permute-start | bytes 1572872 | tf_op jit(solution)/shard_map/ppermute | solution.py:31
  91.9 1.2 add_convert_fusion.3
  93.1 8.0 %collective-permute-start.30 = (bf16[4,256,128]{2,1,0:T(8,128)(2,1)S(1)}, bf16[4,256,128]{2,1,0:T(8,128)(2,1)S(1)}, u32[]{:S(2)}, u32[]{:S(2)}) collective-permute-start(bf16[4,256,128]{2,1,0:T(8,128)(2,1)S(1)} %slice.145), channel_id=1, source_target_pairs={{0,8},{4,12},{8,0},{12,4},{24,16},{28,20},{16,24},{20,28},{32,40},... | collective-permute-start | bytes 786440 | tf_op jit(solution)/shard_map/ppermute | solution.py:31
  101.3 2.6 %collective-permute-start.34 = (bf16[4,256,128]{2,1,0:T(8,128)(2,1)S(1)}, bf16[4,256,128]{2,1,0:T(8,128)(2,1)S(1)}, u32[]{:S(2)}, u32[]{:S(2)}) collective-permute-start(bf16[4,256,128]{2,1,0:T(8,128)(2,1)S(1)} %slice.147), channel_id=1, source_target_pairs={{0,24},{4,28},{8,16},{12,20},{24,0},{28,4},{16,8},{20,12},{32,56},... | collective-permute-start | bytes 786440 | tf_op jit(solution)/shard_map/ppermute | solution.py:31
  104.3 2.5 %collective-permute-start.43 = (bf16[4,256,128]{2,1,0:T(8,128)(2,1)S(1)}, bf16[4,256,128]{2,1,0:T(8,128)(2,1)S(1)}, u32[]{:S(2)}, u32[]{:S(2)}) collective-permute-start(bf16[4,256,128]{2,1,0:T(8,128)(2,1)S(1)} %slice.160), channel_id=1, source_target_pairs={{0,96},{4,100},{8,104},{12,108},{24,120},{28,124},{16,112},{20,116... | collective-permute-start | bytes 786440 | tf_op jit(solution)/shard_map/ppermute | solution.py:31
  107.0 1.9 %collective-permute-start.31 = (bf16[2,256,128]{2,1,0:T(8,128)(2,1)S(1)}, bf16[2,256,128]{2,1,0:T(8,128)(2,1)S(1)}, u32[]{:S(2)}, u32[]{:S(2)}) collective-permute-start(bf16[2,256,128]{2,1,0:T(8,128)(2,1)S(1)} %slice.117), channel_id=1, source_target_pairs={{0,24},{4,28},{8,16},{12,20},{24,0},{28,4},{16,8},{20,12},{32,56},... | collective-permute-start | bytes 393224 | tf_op jit(solution)/shard_map/ppermute | solution.py:31
  109.1 1.4 %collective-permute-start.35 = (bf16[2,256,128]{2,1,0:T(8,128)(2,1)S(1)}, bf16[2,256,128]{2,1,0:T(8,128)(2,1)S(1)}, u32[]{:S(2)}, u32[]{:S(2)}) collective-permute-start(bf16[2,256,128]{2,1,0:T(8,128)(2,1)S(1)} %slice.149), channel_id=1, source_target_pairs={{0,32},{4,36},{8,40},{12,44},{24,56},{28,60},{16,48},{20,52},{32,0... | collective-permute-start | bytes 393224 | tf_op jit(solution)/shard_map/ppermute | solution.py:31
  110.6 2.5 %collective-permute-start.39 = (bf16[2,256,128]{2,1,0:T(8,128)(2,1)S(1)}, bf16[2,256,128]{2,1,0:T(8,128)(2,1)S(1)}, u32[]{:S(2)}, u32[]{:S(2)}) collective-permute-start(bf16[2,256,128]{2,1,0:T(8,128)(2,1)S(1)} %slice.155), channel_id=1, source_target_pairs={{0,96},{4,100},{8,104},{12,108},{24,120},{28,124},{16,112},{20,116... | collective-permute-start | bytes 393224 | tf_op jit(solution)/shard_map/ppermute | solution.py:31
  113.4 1.7 %collective-permute-done.35 = bf16[2,256,128]{2,1,0:T(8,128)(2,1)S(1)} collective-permute-done((bf16[2,256,128]{2,1,0:T(8,128)(2,1)S(1)}, bf16[2,256,128]{2,1,0:T(8,128)(2,1)S(1)}, u32[]{:S(2)}, u32[]{:S(2)}) %collective-permute-start.35) | collective-permute-done | bytes 131104 | tf_op jit(solution)/shard_map/ppermute | solution.py:31
  115.1 1.9 %collective-permute-start.36 = (bf16[1,256,128]{2,1,0:T(8,128)(2,1)S(1)}, bf16[1,256,128]{2,1,0:T(8,128)(2,1)S(1)}, u32[]{:S(2)}, u32[]{:S(2)}) collective-permute-start(bf16[1,256,128]{2,1,0:T(8,128)(2,1)S(1)} %slice.151), channel_id=1, source_target_pairs={{0,96},{4,100},{8,104},{12,108},{24,120},{28,124},{16,112},{20,116... | collective-permute-start | bytes 196616 | tf_op jit(solution)/shard_map/ppermute | solution.py:31
  118.4 2.3 %collective-permute-start.45 = (bf16[1,256,128]{2,1,0:T(8,128)(2,1)S(1)}, bf16[1,256,128]{2,1,0:T(8,128)(2,1)S(1)}, u32[]{:S(2)}, u32[]{:S(2)}) collective-permute-start(bf16[1,256,128]{2,1,0:T(8,128)(2,1)S(1)} %slice.164), channel_id=1, source_target_pairs={{0,24},{4,28},{8,16},{12,20},{24,0},{28,4},{16,8},{20,12},{32,56},... | collective-permute-start | bytes 196616 | tf_op jit(solution)/shard_map/ppermute | solution.py:31
  120.8 1.4 %maximum_select_fusion = bf16[256,2048]{1,0:T(8,128)(2,1)} fusion(bf16[256,1024]{1,0:T(8,128)(2,1)S(1)} %collective-permute-done.32, bf16[256,1024]{1,0:T(8,128)(2,1)S(1)} %copy-done.6, pred[]{:T(512)S(6)} %eq.66), kind=kLoop, calls=%fused_computation | loop fusion | flops 4718592 | bytes 2097153 | tf_op jit(solution)/shard_map/jit(_where)/select_n | solution.py:494
  122.5 1.4 %collective-permute-done.45 = bf16[1,256,128]{2,1,0:T(8,128)(2,1)S(1)} collective-permute-done((bf16[1,256,128]{2,1,0:T(8,128)(2,1)S(1)}, bf16[1,256,128]{2,1,0:T(8,128)(2,1)S(1)}, u32[]{:S(2)}, u32[]{:S(2)}) %collective-permute-start.45) | collective-permute-done | bytes 65568 | tf_op jit(solution)/shard_map/ppermute | solution.py:31
  124.0 2.0 %collective-permute-done.46 = bf16[1,256,128]{2,1,0:T(8,128)(2,1)S(1)} collective-permute-done((bf16[1,256,128]{2,1,0:T(8,128)(2,1)S(1)}, bf16[1,256,128]{2,1,0:T(8,128)(2,1)S(1)}, u32[]{:S(2)}, u32[]{:S(2)}) %collective-permute-start.46) | collective-permute-done | bytes 65568 | tf_op jit(solution)/shard_map/ppermute | solution.py:31
  126.0 0.7 maximum_select_fusion.1
  (150 shorter events, 10.5 us)
Async XLA Ops:
  3.0 2.3 %collective-permute-start = (bf16[256,128]{1,0:T(8,128)(2,1)}, bf16[256,128]{1,0:T(8,128)(2,1)S(1)}, u32[]{:S(2)}, u32[]{:S(2)}) collective-permute-start(bf16[256,128]{1,0:T(8,128)(2,1)} %get-tuple-element.42), channel_id=1, source_target_pairs={{0,4},{4,0},{8,12},{12,8},{16,20},{20,16},{24,28},{28,24},{32,36},... | collective-permute-start | bytes 196616 | tf_op jit(solution)/shard_map/ppermute | solution.py:35
  3.1 9.3 %collective-permute-start.9 = (bf16[256,128]{1,0:T(8,128)(2,1)}, bf16[256,128]{1,0:T(8,128)(2,1)S(1)}, u32[]{:S(2)}, u32[]{:S(2)}) collective-permute-start(bf16[256,128]{1,0:T(8,128)(2,1)} %get-tuple-element.47), channel_id=1, source_target_pairs={{0,4},{4,0},{8,12},{12,8},{16,20},{20,16},{24,28},{28,24},{32,36},... | collective-permute-start | bytes 196616 | tf_op jit(solution)/shard_map/ppermute | solution.py:35
  3.6 16.0 %collective-permute-start.6 = (bf16[1,256,128]{2,1,0:T(8,128)(2,1)}, bf16[1,256,128]{2,1,0:T(8,128)(2,1)S(1)}, u32[]{:S(2)}, u32[]{:S(2)}) collective-permute-start(bf16[1,256,128]{2,1,0:T(8,128)(2,1)} %bitcast.68), channel_id=1, source_target_pairs={{0,8},{4,12},{8,0},{12,4},{24,16},{28,20},{16,24},{20,28},{32,40},... | collective-permute-start | bytes 196616 | tf_op jit(solution)/shard_map/ppermute | solution.py:31
  5.3 9.1 %collective-permute-start.3 = (s32[1,128]{1,0:T(1,128)}, s32[1,128]{1,0:T(1,128)S(1)}, u32[]{:S(2)}, u32[]{:S(2)}) collective-permute-start(s32[1,128]{1,0:T(1,128)} %get-tuple-element.43), channel_id=1, source_target_pairs={{0,3},{1,0},{2,1},{3,2},{4,7},{5,4},{6,5},{7,6},{8,11},{9,8},{10,9... | collective-permute-start | bytes 1544 | tf_op jit(solution)/shard_map/ppermute | solution.py:471
  8.2 6.3 %collective-permute-start.2 = (s32[1,128]{1,0:T(1,128)}, s32[1,128]{1,0:T(1,128)S(1)}, u32[]{:S(2)}, u32[]{:S(2)}) collective-permute-start(s32[1,128]{1,0:T(1,128)} %get-tuple-element.43), channel_id=1, source_target_pairs={{0,2},{1,3},{2,0},{3,1},{4,6},{5,7},{6,4},{7,5},{8,10},{9,11},{10,... | collective-permute-start | bytes 1544 | tf_op jit(solution)/shard_map/ppermute | solution.py:471
  9.0 8.3 %collective-permute-start.1 = (s32[1,128]{1,0:T(1,128)}, s32[1,128]{1,0:T(1,128)S(1)}, u32[]{:S(2)}, u32[]{:S(2)}) collective-permute-start(s32[1,128]{1,0:T(1,128)} %get-tuple-element.43), channel_id=1, source_target_pairs={{0,1},{1,2},{2,3},{3,0},{4,5},{5,6},{6,7},{7,4},{8,9},{9,10},{10,1... | collective-permute-start | bytes 1544 | tf_op jit(solution)/shard_map/ppermute | solution.py:471
  12.4 9.0 %collective-permute-start.8 = (bf16[1,256,128]{2,1,0:T(8,128)(2,1)S(1)}, bf16[1,256,128]{2,1,0:T(8,128)(2,1)S(1)}, u32[]{:S(2)}, u32[]{:S(2)}) collective-permute-start(bf16[1,256,128]{2,1,0:T(8,128)(2,1)S(1)} %bitcast.66), channel_id=1, source_target_pairs={{0,32},{4,36},{8,40},{12,44},{24,56},{28,60},{16,48},{20,52},{32,0... | collective-permute-start | bytes 196616 | tf_op jit(solution)/shard_map/ppermute | solution.py:31
  14.4 40.1 %collective-permute-start.17 = (bf16[3,256,1024]{2,1,0:T(8,128)(2,1)}, bf16[3,256,1024]{2,1,0:T(8,128)(2,1)S(1)}, u32[]{:S(2)}, u32[]{:S(2)}) collective-permute-start(bf16[3,256,1024]{2,1,0:T(8,128)(2,1)} %pack_queries.1), channel_id=1, source_target_pairs={{0,4},{4,0},{8,12},{12,8},{16,20},{20,16},{24,28},{28,24},{32,36},... | collective-permute-start | bytes 4718600 | tf_op jit(solution)/shard_map/ppermute | solution.py:35
  14.4 9.9 %collective-permute-start.10 = (bf16[1,256,128]{2,1,0:T(8,128)(2,1)S(1)}, bf16[1,256,128]{2,1,0:T(8,128)(2,1)S(1)}, u32[]{:S(2)}, u32[]{:S(2)}) collective-permute-start(bf16[1,256,128]{2,1,0:T(8,128)(2,1)S(1)} %bitcast.64), channel_id=1, source_target_pairs={{0,96},{4,100},{8,104},{12,108},{24,120},{28,124},{16,112},{20,116... | collective-permute-start | bytes 196616 | tf_op jit(solution)/shard_map/ppermute | solution.py:31
  17.3 7.1 %collective-permute-start.7 = (bf16[1,256,128]{2,1,0:T(8,128)(2,1)S(1)}, bf16[1,256,128]{2,1,0:T(8,128)(2,1)S(1)}, u32[]{:S(2)}, u32[]{:S(2)}) collective-permute-start(bf16[1,256,128]{2,1,0:T(8,128)(2,1)S(1)} %bitcast.62), channel_id=1, source_target_pairs={{0,24},{4,28},{8,16},{12,20},{24,0},{28,4},{16,8},{20,12},{32,56},... | collective-permute-start | bytes 196616 | tf_op jit(solution)/shard_map/ppermute | solution.py:31
  19.6 1.2 collective-permute-start.4
  20.8 3.5 %collective-permute-start.5 = (s32[1,128]{1,0:T(1,128)S(1)}, s32[1,128]{1,0:T(1,128)S(1)}, u32[]{:S(2)}, u32[]{:S(2)}) collective-permute-start(s32[1,128]{1,0:T(1,128)S(1)} %max.27), channel_id=1, source_target_pairs={{0,8},{4,12},{8,0},{12,4},{24,16},{28,20},{16,24},{20,28},{32,40},... | collective-permute-start | bytes 1544 | tf_op jit(solution)/shard_map/ppermute | solution.py:31
  24.4 5.0 %collective-permute-start.12 = (bf16[2,256,128]{2,1,0:T(8,128)(2,1)S(1)}, bf16[2,256,128]{2,1,0:T(8,128)(2,1)S(1)}, u32[]{:S(2)}, u32[]{:S(2)}) collective-permute-start(bf16[2,256,128]{2,1,0:T(8,128)(2,1)S(1)} %pad_maximum_fusion.7), channel_id=1, source_target_pairs={{0,32},{4,36},{8,40},{12,44},{24,56},{28,60},{16,48},{20,52},{32,0... | collective-permute-start | bytes 393224 | tf_op jit(solution)/shard_map/ppermute | solution.py:31
  25.3 6.2 %collective-permute-start.13 = (bf16[2,256,128]{2,1,0:T(8,128)(2,1)S(1)}, bf16[2,256,128]{2,1,0:T(8,128)(2,1)S(1)}, u32[]{:S(2)}, u32[]{:S(2)}) collective-permute-start(bf16[2,256,128]{2,1,0:T(8,128)(2,1)S(1)} %pad_maximum_fusion.8), channel_id=1, source_target_pairs={{0,96},{4,100},{8,104},{12,108},{24,120},{28,124},{16,112},{20,116... | collective-permute-start | bytes 393224 | tf_op jit(solution)/shard_map/ppermute | solution.py:31
  26.0 5.5 %collective-permute-start.14 = (bf16[2,256,128]{2,1,0:T(8,128)(2,1)S(1)}, bf16[2,256,128]{2,1,0:T(8,128)(2,1)S(1)}, u32[]{:S(2)}, u32[]{:S(2)}) collective-permute-start(bf16[2,256,128]{2,1,0:T(8,128)(2,1)S(1)} %pad_maximum_fusion.9), channel_id=1, source_target_pairs={{0,8},{4,12},{8,0},{12,4},{24,16},{28,20},{16,24},{20,28},{32,40},... | collective-permute-start | bytes 393224 | tf_op jit(solution)/shard_map/ppermute | solution.py:31
  26.7 6.3 %collective-permute-start.11 = (bf16[2,272,128]{2,1,0:T(8,128)(2,1)S(1)}, bf16[2,272,128]{2,1,0:T(8,128)(2,1)S(1)}, u32[]{:S(2)}, u32[]{:S(2)}) collective-permute-start(bf16[2,272,128]{2,1,0:T(8,128)(2,1)S(1)} %pad_maximum_fusion.5), channel_id=1, source_target_pairs={{0,24},{4,28},{8,16},{12,20},{24,0},{28,4},{16,8},{20,12},{32,56},... | collective-permute-start | bytes 417800 | tf_op jit(solution)/shard_map/ppermute | solution.py:31
  29.5 27.9 %copy-start.10 = (s32[4,32]{1,0:T(4,128)S(1)}, s32[4,32]{1,0:T(4,128)}, u32[]{:S(2)}) copy-start(s32[4,32]{1,0:T(4,128)} %constant.126.clone) | copy-start | bytes 1540
  33.2 6.7 %collective-permute-start.15 = (bf16[4,272,128]{2,1,0:T(8,128)(2,1)S(1)}, bf16[4,272,128]{2,1,0:T(8,128)(2,1)}, u32[]{:S(2)}, u32[]{:S(2)}) collective-permute-start(bf16[4,272,128]{2,1,0:T(8,128)(2,1)S(1)} %pad_maximum_fusion), channel_id=1, source_target_pairs={{0,32},{4,36},{8,40},{12,44},{24,56},{28,60},{16,48},{20,52},{32,0... | collective-permute-start | bytes 835592 | tf_op jit(solution)/shard_map/ppermute | solution.py:31
  34.0 9.3 %collective-permute-start.21 = (bf16[4,256,128]{2,1,0:T(8,128)(2,1)S(1)}, bf16[4,256,128]{2,1,0:T(8,128)(2,1)S(1)}, u32[]{:S(2)}, u32[]{:S(2)}) collective-permute-start(bf16[4,256,128]{2,1,0:T(8,128)(2,1)S(1)} %pad_maximum_fusion.1), channel_id=1, source_target_pairs={{0,96},{4,100},{8,104},{12,108},{24,120},{28,124},{16,112},{20,116... | collective-permute-start | bytes 786440 | tf_op jit(solution)/shard_map/ppermute | solution.py:31
  36.5 7.9 %collective-permute-start.22 = (bf16[4,256,128]{2,1,0:T(8,128)(2,1)S(1)}, bf16[4,256,128]{2,1,0:T(8,128)(2,1)S(1)}, u32[]{:S(2)}, u32[]{:S(2)}) collective-permute-start(bf16[4,256,128]{2,1,0:T(8,128)(2,1)S(1)} %pad_maximum_fusion.2), channel_id=1, source_target_pairs={{0,8},{4,12},{8,0},{12,4},{24,16},{28,20},{16,24},{20,28},{32,40},... | collective-permute-start | bytes 786440 | tf_op jit(solution)/shard_map/ppermute | solution.py:31
  36.9 9.3 %collective-permute-start.18 = (bf16[4,256,128]{2,1,0:T(8,128)(2,1)S(1)}, bf16[4,256,128]{2,1,0:T(8,128)(2,1)}, u32[]{:S(2)}, u32[]{:S(2)}) collective-permute-start(bf16[4,256,128]{2,1,0:T(8,128)(2,1)S(1)} %pad_maximum_fusion.2), channel_id=1, source_target_pairs={{0,96},{4,100},{8,104},{12,108},{24,120},{28,124},{16,112},{20,116... | collective-permute-start | bytes 786440 | tf_op jit(solution)/shard_map/ppermute | solution.py:31
  40.0 9.5 %collective-permute-start.23 = (bf16[4,256,128]{2,1,0:T(8,128)(2,1)S(1)}, bf16[4,256,128]{2,1,0:T(8,128)(2,1)S(1)}, u32[]{:S(2)}, u32[]{:S(2)}) collective-permute-start(bf16[4,256,128]{2,1,0:T(8,128)(2,1)S(1)} %pad_maximum_fusion.3), channel_id=1, source_target_pairs={{0,24},{4,28},{8,16},{12,20},{24,0},{28,4},{16,8},{20,12},{32,56},... | collective-permute-start | bytes 786440 | tf_op jit(solution)/shard_map/ppermute | solution.py:31
  43.3 7.3 %collective-permute-start.19 = (bf16[4,256,128]{2,1,0:T(8,128)(2,1)S(1)}, bf16[4,256,128]{2,1,0:T(8,128)(2,1)}, u32[]{:S(2)}, u32[]{:S(2)}) collective-permute-start(bf16[4,256,128]{2,1,0:T(8,128)(2,1)S(1)} %pad_maximum_fusion.3), channel_id=1, source_target_pairs={{0,8},{4,12},{8,0},{12,4},{24,16},{28,20},{16,24},{20,28},{32,40},... | collective-permute-start | bytes 786440 | tf_op jit(solution)/shard_map/ppermute | solution.py:31
  44.5 9.2 %collective-permute-start.20 = (bf16[4,256,128]{2,1,0:T(8,128)(2,1)S(1)}, bf16[4,256,128]{2,1,0:T(8,128)(2,1)}, u32[]{:S(2)}, u32[]{:S(2)}) collective-permute-start(bf16[4,256,128]{2,1,0:T(8,128)(2,1)S(1)} %pad_maximum_fusion.4), channel_id=1, source_target_pairs={{0,24},{4,28},{8,16},{12,20},{24,0},{28,4},{16,8},{20,12},{32,56},... | collective-permute-start | bytes 786440 | tf_op jit(solution)/shard_map/ppermute | solution.py:31
  46.2 8.3 %collective-permute-start.16 = (s32[1,128]{1,0:T(1,128)S(1)}, s32[1,128]{1,0:T(1,128)S(1)}, u32[]{:S(2)}, u32[]{:S(2)}) collective-permute-start(s32[1,128]{1,0:T(1,128)S(1)} %bitcast_maximum_fusion), channel_id=1, source_target_pairs={{0,96},{4,100},{8,104},{12,108},{24,120},{28,124},{16,112},{20,116... | collective-permute-start | bytes 1544 | tf_op jit(solution)/shard_map/ppermute | solution.py:31
  50.2 16.4 %collective-permute-start.24 = (bf16[4,256,128]{2,1,0:T(8,128)(2,1)S(1)}, bf16[4,256,128]{2,1,0:T(8,128)(2,1)}, u32[]{:S(2)}, u32[]{:S(2)}) collective-permute-start(bf16[4,256,128]{2,1,0:T(8,128)(2,1)S(1)} %pad_maximum_fusion.4), channel_id=1, source_target_pairs={{0,32},{4,36},{8,40},{12,44},{24,56},{28,60},{16,48},{20,52},{32,0... | collective-permute-start | bytes 786440 | tf_op jit(solution)/shard_map/ppermute | solution.py:31
  50.6 16.0 %collective-permute-start.26 = (bf16[4,256,128]{2,1,0:T(8,128)(2,1)}, bf16[4,256,128]{2,1,0:T(8,128)(2,1)}, u32[]{:S(2)}, u32[]{:S(2)}) collective-permute-start(bf16[4,256,128]{2,1,0:T(8,128)(2,1)} %collective-permute-done.18), channel_id=1, source_target_pairs={{0,8},{4,12},{8,0},{12,4},{24,16},{28,20},{16,24},{20,28},{32,40},... | collective-permute-start | bytes 786440 | tf_op jit(solution)/shard_map/ppermute | solution.py:31
  53.6 13.0 %collective-permute-start.27 = (bf16[4,256,128]{2,1,0:T(8,128)(2,1)}, bf16[4,256,128]{2,1,0:T(8,128)(2,1)}, u32[]{:S(2)}, u32[]{:S(2)}) collective-permute-start(bf16[4,256,128]{2,1,0:T(8,128)(2,1)} %collective-permute-done.19), channel_id=1, source_target_pairs={{0,24},{4,28},{8,16},{12,20},{24,0},{28,4},{16,8},{20,12},{32,56},... | collective-permute-start | bytes 786440 | tf_op jit(solution)/shard_map/ppermute | solution.py:31
  54.5 12.1 %collective-permute-start.28 = (bf16[4,256,128]{2,1,0:T(8,128)(2,1)}, bf16[4,256,128]{2,1,0:T(8,128)(2,1)}, u32[]{:S(2)}, u32[]{:S(2)}) collective-permute-start(bf16[4,256,128]{2,1,0:T(8,128)(2,1)} %collective-permute-done.20), channel_id=1, source_target_pairs={{0,32},{4,36},{8,40},{12,44},{24,56},{28,60},{16,48},{20,52},{32,0... | collective-permute-start | bytes 786440 | tf_op jit(solution)/shard_map/ppermute | solution.py:31
  54.5 12.1 %collective-permute-start.25 = (bf16[4,256,128]{2,1,0:T(8,128)(2,1)S(1)}, bf16[4,256,128]{2,1,0:T(8,128)(2,1)}, u32[]{:S(2)}, u32[]{:S(2)}) collective-permute-start(bf16[4,256,128]{2,1,0:T(8,128)(2,1)S(1)} %slice.143), channel_id=1, source_target_pairs={{0,96},{4,100},{8,104},{12,108},{24,120},{28,124},{16,112},{20,116... | collective-permute-start | bytes 786440 | tf_op jit(solution)/shard_map/ppermute | solution.py:31
  81.1 10.8 %collective-permute-start.29 = (bf16[8,256,128]{2,1,0:T(8,128)(2,1)}, bf16[8,256,128]{2,1,0:T(8,128)(2,1)}, u32[]{:S(2)}, u32[]{:S(2)}) collective-permute-start(bf16[8,256,128]{2,1,0:T(8,128)(2,1)} %get-tuple-element.66), channel_id=1, source_target_pairs={{0,96},{4,100},{8,104},{12,108},{24,120},{28,124},{16,112},{20,116... | collective-permute-start | bytes 1572872 | tf_op jit(solution)/shard_map/ppermute | solution.py:31
  81.2 19.9 %collective-permute-start.33 = (bf16[8,256,128]{2,1,0:T(8,128)(2,1)}, bf16[8,256,128]{2,1,0:T(8,128)(2,1)S(1)}, u32[]{:S(2)}, u32[]{:S(2)}) collective-permute-start(bf16[8,256,128]{2,1,0:T(8,128)(2,1)} %get-tuple-element.73), channel_id=1, source_target_pairs={{0,8},{4,12},{8,0},{12,4},{24,16},{28,20},{16,24},{20,28},{32,40},... | collective-permute-start | bytes 1572872 | tf_op jit(solution)/shard_map/ppermute | solution.py:31
  89.3 14.6 %collective-permute-start.37 = (bf16[8,256,128]{2,1,0:T(8,128)(2,1)}, bf16[8,256,128]{2,1,0:T(8,128)(2,1)S(1)}, u32[]{:S(2)}, u32[]{:S(2)}) collective-permute-start(bf16[8,256,128]{2,1,0:T(8,128)(2,1)} %get-tuple-element.75), channel_id=1, source_target_pairs={{0,24},{4,28},{8,16},{12,20},{24,0},{28,4},{16,8},{20,12},{32,56},... | collective-permute-start | bytes 1572872 | tf_op jit(solution)/shard_map/ppermute | solution.py:31
  91.4 12.7 %collective-permute-start.42 = (bf16[8,256,128]{2,1,0:T(8,128)(2,1)}, bf16[8,256,128]{2,1,0:T(8,128)(2,1)S(1)}, u32[]{:S(2)}, u32[]{:S(2)}) collective-permute-start(bf16[8,256,128]{2,1,0:T(8,128)(2,1)} %get-tuple-element.78), channel_id=1, source_target_pairs={{0,32},{4,36},{8,40},{12,44},{24,56},{28,60},{16,48},{20,52},{32,0... | collective-permute-start | bytes 1572872 | tf_op jit(solution)/shard_map/ppermute | solution.py:31
  93.1 13.8 %collective-permute-start.30 = (bf16[4,256,128]{2,1,0:T(8,128)(2,1)S(1)}, bf16[4,256,128]{2,1,0:T(8,128)(2,1)S(1)}, u32[]{:S(2)}, u32[]{:S(2)}) collective-permute-start(bf16[4,256,128]{2,1,0:T(8,128)(2,1)S(1)} %slice.145), channel_id=1, source_target_pairs={{0,8},{4,12},{8,0},{12,4},{24,16},{28,20},{16,24},{20,28},{32,40},... | collective-permute-start | bytes 786440 | tf_op jit(solution)/shard_map/ppermute | solution.py:31
  101.3 7.7 %collective-permute-start.34 = (bf16[4,256,128]{2,1,0:T(8,128)(2,1)S(1)}, bf16[4,256,128]{2,1,0:T(8,128)(2,1)S(1)}, u32[]{:S(2)}, u32[]{:S(2)}) collective-permute-start(bf16[4,256,128]{2,1,0:T(8,128)(2,1)S(1)} %slice.147), channel_id=1, source_target_pairs={{0,24},{4,28},{8,16},{12,20},{24,0},{28,4},{16,8},{20,12},{32,56},... | collective-permute-start | bytes 786440 | tf_op jit(solution)/shard_map/ppermute | solution.py:31
  104.1 6.5 %collective-permute-start.38 = (bf16[4,256,128]{2,1,0:T(8,128)(2,1)S(1)}, bf16[4,256,128]{2,1,0:T(8,128)(2,1)S(1)}, u32[]{:S(2)}, u32[]{:S(2)}) collective-permute-start(bf16[4,256,128]{2,1,0:T(8,128)(2,1)S(1)} %slice.153), channel_id=1, source_target_pairs={{0,32},{4,36},{8,40},{12,44},{24,56},{28,60},{16,48},{20,52},{32,0... | collective-permute-start | bytes 786440 | tf_op jit(solution)/shard_map/ppermute | solution.py:31
  104.3 8.8 %collective-permute-start.43 = (bf16[4,256,128]{2,1,0:T(8,128)(2,1)S(1)}, bf16[4,256,128]{2,1,0:T(8,128)(2,1)S(1)}, u32[]{:S(2)}, u32[]{:S(2)}) collective-permute-start(bf16[4,256,128]{2,1,0:T(8,128)(2,1)S(1)} %slice.160), channel_id=1, source_target_pairs={{0,96},{4,100},{8,104},{12,108},{24,120},{28,124},{16,112},{20,116... | collective-permute-start | bytes 786440 | tf_op jit(solution)/shard_map/ppermute | solution.py:31
  107.0 13.7 %collective-permute-start.31 = (bf16[2,256,128]{2,1,0:T(8,128)(2,1)S(1)}, bf16[2,256,128]{2,1,0:T(8,128)(2,1)S(1)}, u32[]{:S(2)}, u32[]{:S(2)}) collective-permute-start(bf16[2,256,128]{2,1,0:T(8,128)(2,1)S(1)} %slice.117), channel_id=1, source_target_pairs={{0,24},{4,28},{8,16},{12,20},{24,0},{28,4},{16,8},{20,12},{32,56},... | collective-permute-start | bytes 393224 | tf_op jit(solution)/shard_map/ppermute | solution.py:31
  108.9 11.8 %collective-permute-start.32 = (bf16[256,1024]{1,0:T(8,128)(2,1)S(1)}, bf16[256,1024]{1,0:T(8,128)(2,1)S(1)}, u32[]{:S(2)}, u32[]{:S(2)}) collective-permute-start(bf16[256,1024]{1,0:T(8,128)(2,1)S(1)} %copy-done.15), channel_id=1, source_target_pairs={{0,4},{4,0},{8,12},{12,8},{16,20},{20,16},{24,28},{28,24},{32,36},... | collective-permute-start | bytes 1572872 | tf_op jit(solution)/shard_map/ppermute | solution.py:35
  109.1 5.9 %collective-permute-start.35 = (bf16[2,256,128]{2,1,0:T(8,128)(2,1)S(1)}, bf16[2,256,128]{2,1,0:T(8,128)(2,1)S(1)}, u32[]{:S(2)}, u32[]{:S(2)}) collective-permute-start(bf16[2,256,128]{2,1,0:T(8,128)(2,1)S(1)} %slice.149), channel_id=1, source_target_pairs={{0,32},{4,36},{8,40},{12,44},{24,56},{28,60},{16,48},{20,52},{32,0... | collective-permute-start | bytes 393224 | tf_op jit(solution)/shard_map/ppermute | solution.py:31
  110.6 6.9 %collective-permute-start.39 = (bf16[2,256,128]{2,1,0:T(8,128)(2,1)S(1)}, bf16[2,256,128]{2,1,0:T(8,128)(2,1)S(1)}, u32[]{:S(2)}, u32[]{:S(2)}) collective-permute-start(bf16[2,256,128]{2,1,0:T(8,128)(2,1)S(1)} %slice.155), channel_id=1, source_target_pairs={{0,96},{4,100},{8,104},{12,108},{24,120},{28,124},{16,112},{20,116... | collective-permute-start | bytes 393224 | tf_op jit(solution)/shard_map/ppermute | solution.py:31
  113.3 5.0 %collective-permute-start.44 = (bf16[2,256,128]{2,1,0:T(8,128)(2,1)S(1)}, bf16[2,256,128]{2,1,0:T(8,128)(2,1)S(1)}, u32[]{:S(2)}, u32[]{:S(2)}) collective-permute-start(bf16[2,256,128]{2,1,0:T(8,128)(2,1)S(1)} %slice.162), channel_id=1, source_target_pairs={{0,8},{4,12},{8,0},{12,4},{24,16},{28,20},{16,24},{20,28},{32,40},... | collective-permute-start | bytes 393224 | tf_op jit(solution)/shard_map/ppermute | solution.py:31
  115.1 5.6 %collective-permute-start.36 = (bf16[1,256,128]{2,1,0:T(8,128)(2,1)S(1)}, bf16[1,256,128]{2,1,0:T(8,128)(2,1)S(1)}, u32[]{:S(2)}, u32[]{:S(2)}) collective-permute-start(bf16[1,256,128]{2,1,0:T(8,128)(2,1)S(1)} %slice.151), channel_id=1, source_target_pairs={{0,96},{4,100},{8,104},{12,108},{24,120},{28,124},{16,112},{20,116... | collective-permute-start | bytes 196616 | tf_op jit(solution)/shard_map/ppermute | solution.py:31
  117.6 6.4 %collective-permute-start.41 = (bf16[1,256,128]{2,1,0:T(8,128)(2,1)S(1)}, bf16[1,256,128]{2,1,0:T(8,128)(2,1)S(1)}, u32[]{:S(2)}, u32[]{:S(2)}) collective-permute-start(bf16[1,256,128]{2,1,0:T(8,128)(2,1)S(1)} %get-tuple-element.88), channel_id=1, source_target_pairs={{0,12},{4,8},{8,4},{12,0},{24,20},{28,16},{16,28},{20,24},{32,44},... | collective-permute-start | bytes 196616 | tf_op jit(solution)/shard_map/ppermute | solution.py:31
  118.4 5.6 %collective-permute-start.45 = (bf16[1,256,128]{2,1,0:T(8,128)(2,1)S(1)}, bf16[1,256,128]{2,1,0:T(8,128)(2,1)S(1)}, u32[]{:S(2)}, u32[]{:S(2)}) collective-permute-start(bf16[1,256,128]{2,1,0:T(8,128)(2,1)S(1)} %slice.164), channel_id=1, source_target_pairs={{0,24},{4,28},{8,16},{12,20},{24,0},{28,4},{16,8},{20,12},{32,56},... | collective-permute-start | bytes 196616 | tf_op jit(solution)/shard_map/ppermute | solution.py:31
  122.2 3.8 %collective-permute-start.46 = (bf16[1,256,128]{2,1,0:T(8,128)(2,1)S(1)}, bf16[1,256,128]{2,1,0:T(8,128)(2,1)S(1)}, u32[]{:S(2)}, u32[]{:S(2)}) collective-permute-start(bf16[1,256,128]{2,1,0:T(8,128)(2,1)S(1)} %get-tuple-element.85), channel_id=1, source_target_pairs={{0,36},{4,32},{8,44},{12,40},{24,60},{28,56},{16,52},{20,48},{32,4... | collective-permute-start | bytes 196616 | tf_op jit(solution)/shard_map/ppermute | solution.py:31
  122.3 3.7 %collective-permute-start.40 = (bf16[2,1,256,128]{3,2,1,0:T(8,128)(2,1)S(1)}, bf16[2,1,256,128]{3,2,1,0:T(8,128)(2,1)S(1)}, u32[]{:S(2)}, u32[]{:S(2)}) collective-permute-start(bf16[2,1,256,128]{3,2,1,0:T(8,128)(2,1)S(1)} %pad_maximum_fusion.10), channel_id=1, source_target_pairs={{0,4},{4,0},{8,12},{12,8},{16,20},{20,16},{24,28},{28,24},{32,36},... | collective-permute-start | bytes 393224 | tf_op jit(solution)/shard_map/ppermute | solution.py:35
  (15 other events, 196.2 us)
